TPU v7x, 128 devices: a whole 4x4x4 slice. The times are simulated.
128 devices in a mesh: node: 32 (over z, y, x_lo), local: 2 (over core), section: 2 (over x_hi).
Axes of the slice: x: 4 (x_hi: 2, x_lo: 2; x = x_hi * 2 + x_lo), y: 4, z: 4, core: 2. Of those that a mesh axis runs over, the one named last changes fastest.
Arguments:
- tokens: bfloat16 [2, 4096, 4096], P('section', 'node', 'local'), may hold values from -6 to 6
- expert_ids: int32 [2, 4096, 8], P('section', 'node'), may hold values from 0 to 31, all different within a row; in each aligned block of 128 rows (0 to 127, 128 to 255, ..., all dimensions but the last counted through in order) at most 64 rows name the same one
- gate_weights: float32 [2, 4096, 8], P('section', 'node'), may hold values from 0.1 to 1
- expert_node: int32 [2, 32], P('section'), may hold values from 0 to 31, each once within a row
- w_gate: bfloat16 [2, 32, 4096, 1024], P('section', 'node', None, 'local'), may hold values from -0.09375 to 0.09375
- w_up: bfloat16 [2, 32, 4096, 1024], P('section', 'node', None, 'local'), may hold values from -0.09375 to 0.09375
- w_down: bfloat16 [2, 32, 1024, 4096], P('section', 'node', 'local'), may hold values from -0.25 to 0.25
Outputs:
- mixed: bfloat16 [2, 4096, 4096], P('section', 'node', 'local')
Inputs may be any that keep to these rules, and one draw needn't show every extreme that they name: `expert_ids`: in each block of 128 rows of one segment (the rows of one node index) no expert is chosen by more than 64 rows, a bound that some block reaches; the 8 experts of a token differ. `expert_node`: each segment's row names every node index once.
All inputs are finite; a program needn't handle non-finite values.
Results may differ from a plain program's by a relative error of at most 0.0061.
Values may be sent and summed in bfloat16 or wider, within the bound.
A program may use at most 128 MiB of HBM per device.

v0:
```python
import jax
import jax.numpy as jnp
from jax import lax
from jax.sharding import PartitionSpec as P


def from_behind(value, axis, steps):
    count = lax.axis_size(axis)
    pairs = [(source, (source + steps) % count) for source in range(count)]
    return lax.ppermute(value, axis, pairs)


def body(tokens, expert_ids, gate_weights, expert_node, w_gate, w_up, w_down):
    ids = expert_ids[0].reshape(-1)
    pairs = ids.shape[0]
    tok_rows = tokens.shape[1]
    topk_count = expert_ids.shape[2]
    expert_total = expert_node.shape[1]
    feat_share = tokens.shape[2]
    capacity = min(tok_rows, 2 * tok_rows * topk_count // expert_total)
    onehot = (ids[:, None] == jnp.arange(expert_total, dtype=jnp.int32)[None, :]).astype(jnp.int32)
    slot = jnp.sum((jnp.cumsum(onehot, axis=0) - 1) * onehot, axis=1)
    home = jnp.sum(onehot * expert_node[0][None, :], axis=1)
    local_row = jnp.arange(pairs, dtype=jnp.int32) // topk_count
    table = jnp.full((expert_total, capacity), tok_rows, jnp.int32).at[home, slot].set(local_row)
    own_rows = tokens[0]
    padded = jnp.concatenate([own_rows, jnp.zeros((1, feat_share), own_rows.dtype)], axis=0)
    outgoing = padded[table]
    gate_cols = w_gate[0, 0]
    up_cols = w_up[0, 0]
    down_rows = w_down[0, 0]
    row_total = expert_total * capacity
    arrived = lax.all_to_all(outgoing, "node", split_axis=0, concat_axis=0, tiled=True)
    arrived_rows = arrived.reshape(row_total, feat_share)
    piece = lax.all_gather(arrived_rows, "local", axis=1, tiled=True)
    gate_acc = jnp.dot(piece, gate_cols, preferred_element_type=jnp.float32)
    up_acc = jnp.dot(piece, up_cols, preferred_element_type=jnp.float32)
    hidden = (jax.nn.silu(gate_acc) * up_acc).astype(jnp.bfloat16)
    partial_out = jnp.dot(hidden, down_rows, preferred_element_type=jnp.float32).astype(
        jnp.bfloat16
    )
    partial_out = partial_out.reshape(expert_total, capacity, down_rows.shape[1])
    summed = lax.psum_scatter(
        partial_out.astype(jnp.float32).astype(jnp.bfloat16),
        "local",
        scatter_dimension=2,
        tiled=True,
    )
    results = lax.all_to_all(summed, "node", split_axis=0, concat_axis=0, tiled=True)
    flat_results = results.reshape(row_total, feat_share)
    picked = flat_results[home * capacity + slot].astype(jnp.float32)
    picked = picked.reshape(tok_rows, topk_count, feat_share)
    weighted = jnp.sum(picked * gate_weights[0][:, :, None], axis=1)
    layer_out = (own_rows.astype(jnp.float32) + weighted).astype(jnp.bfloat16)
    return from_behind(layer_out[None], "section", 1)


def solution(mesh):
    in_specs = (
        P("section", "node", "local"),
        P("section", "node", None),
        P("section", "node", None),
        P("section", None),
        P("section", "node", None, "local"),
        P("section", "node", None, "local"),
        P("section", "node", "local", None),
    )
    out_specs = P("section", "node", "local")
    return jax.shard_map(body, mesh=mesh, in_specs=in_specs, out_specs=out_specs, check_vma=False)
```

profile of v0, /device:TPU:40, one launch (start us, length us, event | category | flops | bytes accessed | tf_op | source)
XLA Modules:
  0.0 438.7 jit_solution(15767488512879851209)
XLA Ops:
  6.5 0.8 copy.9
  7.5 9.0 %reduce-window.6 = s32[32,8,128]{2,1,0:T(8,128)S(1)} reduce-window(s32[32,8,128]{2,1,0:T(8,128)S(1)} %fusion.14, s32[]{:T(128)} %constant.34.clone.1), window={size=1x1x128 pad=0_0x0_0x127_0}, to_apply=%region_1.2 | reduce-window | flops 4161536 | bytes 262148 | tf_op jit(solution)/shard_map/reduce-window
  16.6 0.1 copy.11
  16.9 0.1 add_add_fusion
  17.0 0.7 select_reduce_fusion
  17.8 0.7 multiply_reduce_fusion
  18.5 0.7 and_reduce_fusion
  19.3 4.3 scatter_custom_fusion
  23.8 1.1 concatenate.6
  24.9 11.0 %gather_fusion = bf16[2048,2048]{1,0:T(8,128)(2,1)} fusion(bf16[129,2048]{1,0:T(8,128)(2,1)S(1)} %concatenate.6, s32[2048]{0:T(1024)S(1)} %broadcast_clamp_fusion), kind=kCustom, calls=%fused_computation | custom fusion | bytes 16785408 | tf_op jit(solution)/shard_map/gather | solution.py:28
  35.9 102.7 %all_to_all.10 = bf16[32,64,2048]{2,1,0:T(8,128)(2,1)} all-to-all(bf16[32,64,2048]{2,1,0:T(8,128)(2,1)} %bitcast.46), channel_id=1, replica_groups=mesh['node'=32,'local'=2,'section'=2] {'node'}, dimensions={0} | all-to-all | bytes 16777216 | tf_op jit(solution)/shard_map/all_to_all | solution.py:33
  138.6 32.9 %all-gather.2.cloned.1.call-done = bf16[2048,4096]{1,0:T(8,128)(2,1)} async-done(((bf16[2048,2048]{1,0:T(8,128)(2,1)}), bf16[2048,4096]{1,0:T(8,128)(2,1)}) %all-gather.2.cloned.1.call-update) | async-done | bytes 16777232 | tf_op jit(solution)/shard_map/all_gather | solution.py:35
  171.5 14.9 %fusion.4 = f32[2048,512]{1,0:T(8,128)} fusion(bf16[2048,4096]{1,0:T(8,128)(2,1)} %all-gather.2.cloned.1.call-done, bf16[1,1,4096,512]{3,2,1,0:T(8,128)(2,1)} %param.11), kind=kOutput, calls=%fused_computation.9 | convolution fusion | flops 8589934592 | bytes 25165824 | tf_op jit(solution)/shard_map/dot_general | solution.py:36
  186.4 26.1 %convolution_convert_fusion = bf16[2048,4096]{1,0:T(8,128)(2,1)} fusion(bf16[1,1,512,4096]{3,2,1,0:T(8,128)(2,1)} %param.13, f32[2048,512]{1,0:T(8,128)} %fusion.4, bf16[2048,4096]{1,0:T(8,128)(2,1)} %all-gather.2.cloned.1.call-done, bf16[1,1,4096,512]{3,2,1,0:T(8,128)(2,1)} %param.12), kind=kOutput, calls=%fused_computation.3 | convolution fusion | flops 17194549248 | bytes 46137344 | tf_op jit(solution)/shard_map/dot_general | solution.py:39
  212.5 30.5 %reduce-scatter.2.cloned.1.call-done = bf16[32,64,2048]{2,1,0:T(8,128)(2,1)} async-done(((bf16[32,64,4096]{2,1,0:T(8,128)(2,1)}), bf16[32,64,2048]{2,1,0:T(8,128)(2,1)}) %reduce-scatter.2.cloned.1.call-update) | async-done | bytes 8388624 | tf_op jit(solution)/shard_map/reduce_scatter | solution.py:43
  243.0 8.4 %all-to-all-start.1 = ((bf16[32,64,2048]{2,1,0:T(8,128)(2,1)}), bf16[32,64,2048]{2,1,0:T(8,128)(2,1)}, u32[]{:S(2)}, u32[]{:S(2)}) async-start(bf16[32,64,2048]{2,1,0:T(8,128)(2,1)} %reduce-scatter.2.cloned.1.call-done), calls=%async_computation.2 | async-start | bytes 16777216 | tf_op jit(solution)/shard_map/all_to_all | solution.py:49
  251.5 0.1 copy.13
  251.6 145.0 %all-to-all-done.1 = bf16[32,64,2048]{2,1,0:T(8,128)(2,1)} async-done(((bf16[32,64,2048]{2,1,0:T(8,128)(2,1)}), bf16[32,64,2048]{2,1,0:T(8,128)(2,1)}, u32[]{:S(2)}, u32[]{:S(2)}) %all-to-all-start.1) | async-done | bytes 8388640 | tf_op jit(solution)/shard_map/all_to_all | solution.py:49
  396.5 13.3 %gather_fusion.1 = bf16[1024,2048]{1,0:T(8,128)(2,1)} fusion(bf16[2048,2048]{1,0:T(8,128)(2,1)} %bitcast.12, s32[1024]{0:T(1024)S(1)} %broadcast_clamp_fusion.1), kind=kCustom, calls=%fused_computation.1 | custom fusion | bytes 8392704 | tf_op jit(solution)/shard_map/gather | solution.py:51
  409.8 6.6 %fusion = f32[128,2048]{1,0:T(8,128)S(1)} fusion(bf16[1024,2048]{1,0:T(8,128)(2,1)} %gather_fusion.1, f32[128,8]{1,0:T(8,128)S(1)} %copy.13), kind=kLoop, calls=%fused_computation.5 | loop fusion | flops 6029312 | bytes 5246976 | tf_op jit(solution)/shard_map/reduce_sum | solution.py:53
  416.4 0.1 fusion.11
  416.5 2.8 collective-permute-start
  419.3 11.8 %collective-permute-done = bf16[1,128,2048]{2,1,0:T(8,128)(2,1)S(1)} collective-permute-done((bf16[1,128,2048]{2,1,0:T(8,128)(2,1)S(1)}, bf16[1,128,2048]{2,1,0:T(8,128)(2,1)S(1)}, u32[]{:S(2)}, u32[]{:S(2)}) %collective-permute-start) | collective-permute-done | bytes 524320 | tf_op jit(solution)/shard_map/ppermute | solution.py:10
  431.1 0.8 copy.17
  (22 shorter events, 0.7 us)
Async XLA Ops:
  6.5 164.9 %all-gather.2.cloned.1.call-start = ((), (), s32[]{:S(2)}) async-start(), calls=%async_computation.3 | async-start | bytes 25165824 | tf_op jit(solution)/shard_map/all_gather | solution.py:35
  138.6 104.4 %reduce-scatter.2.cloned.1.call-start = ((), (), s32[]{:S(2)}) async-start(), calls=%async_computation.4 | async-start | bytes 25165824 | tf_op jit(solution)/shard_map/reduce_scatter | solution.py:43
  212.5 39.0 %copy-start.1 = (f32[1,128,8]{1,2,0:T(8,128)S(1)}, f32[1,128,8]{1,2,0:T(8,128)}, u32[]{:S(2)}) copy-start(f32[1,128,8]{1,2,0:T(8,128)} %param.9) | copy-start | bytes 12292
  243.0 153.5 %all-to-all-start.1 = ((bf16[32,64,2048]{2,1,0:T(8,128)(2,1)}), bf16[32,64,2048]{2,1,0:T(8,128)(2,1)}, u32[]{:S(2)}, u32[]{:S(2)}) async-start(bf16[32,64,2048]{2,1,0:T(8,128)(2,1)} %reduce-scatter.2.cloned.1.call-done), calls=%async_computation.2 | async-start | bytes 16777216 | tf_op jit(solution)/shard_map/all_to_all | solution.py:49
  409.8 6.6 %copy-start = (bf16[1,128,2048]{2,1,0:T(8,128)(2,1)S(1)}, bf16[1,128,2048]{2,1,0:T(8,128)(2,1)}, u32[]{:S(2)}) copy-start(bf16[1,128,2048]{2,1,0:T(8,128)(2,1)} %param.7) | copy-start | bytes 1572868
  416.5 14.5 %collective-permute-start = (bf16[1,128,2048]{2,1,0:T(8,128)(2,1)S(1)}, bf16[1,128,2048]{2,1,0:T(8,128)(2,1)S(1)}, u32[]{:S(2)}, u32[]{:S(2)}) collective-permute-start(bf16[1,128,2048]{2,1,0:T(8,128)(2,1)S(1)} %fusion.11), channel_id=1, source_target_pairs={{0,1},{1,0},{2,3},{3,2},{4,5},{5,4},{6,7},{7,6},{8,9},{9,8},{10,11... | collective-permute-start | bytes 1572872 | tf_op jit(solution)/shard_map/ppermute | solution.py:10
Sparse Core Ops, SparseCore 0:
  138.7 32.7 all-gather.1
  212.6 30.3 reduce-scatter.1
where the time goes:
time: 439 us
  waiting for transfers between devices  220 us (50%)
  blocking collectives  103 us (23%)
  matrix products  41 us (9%)
  local copies, waits for them, and re-layouts  32 us (7%)
  other arithmetic  18.1 us (4%)
  between operations  13.5 us (3%)
  starting transfers between devices  11.2 us (3%)
    all_to_all x1, waiting for transfers between devices, body(): lax.all_to_all(summed, 'node', split_axis=0, concat_axis=0, tiled=True)  145 us
    all_to_all x1, blocking collectives, body(): lax.all_to_all(outgoing, 'node', split_axis=0, concat_axis=0, tiled=True)  103 us
    all_gather x1, waiting for transfers between devices, body(): piece = lax.all_gather(arrived_rows, 'local', axis=1, tiled=True)  32.9 us
    reduce_scatter x1, waiting for transfers between devices, body(): lax.psum_scatter(partial_out.astype(jnp.float32).astype(jnp.bfloat16), 'l...  30.5 us
    dot_general x1, matrix products, body(): jnp.dot(hidden, down_rows, preferred_element_type=jnp.float32)  26.1 us
    dot_general x1, matrix products, body(): gate_acc = jnp.dot(piece, gate_cols, preferred_element_type=jnp.float32)  14.9 us
    gather x1, local copies, waits for them, and re-layouts, body(): picked = flat_results[home * capacity + slot].astype(jnp.float32)  13.3 us
    ppermute x1, waiting for transfers between devices, from_behind(): return lax.ppermute(value, axis, pairs)  11.8 us
  transfers between devices with their start and end apart: 4, of which 4 were waited for; matrix products, arithmetic and copies ran while one was open for 0% of the time, Pallas kernels for 0%

commit v1 on v0

v1 whole, which is shorter than its diff:
```python
import jax
import jax.numpy as jnp
from jax import lax
from jax.experimental import pallas as pl
from jax.experimental.pallas import tpu as pltpu
from jax.sharding import PartitionSpec as P

MESH = pl.DeviceIdType.MESH
BF = jnp.bfloat16
F32 = jnp.float32
RING = 4
CAP = 64
CHUNKS = 8
STAGES = 3
KEEP = 4


def kernel(ids_ref, gates_ref, place_ref, tok, wg_hbm, wu_hbm, wd_hbm, out,
           blocks, aux, pick, spread, staged, rows, rows_x, transit, acc_g, acc_u, wg, wu, wd, hid, hid_x,
           far, kept, far_in, near, near_in, done,
           w_sem, aux_s, aux_r, wd_s, wd_r, d_s, d_r, l_s, l_r, h_s, h_r, c_s, c_r, ready_q, ready_x):
    n_tok, feats = tok.shape
    width = feats // CHUNKS
    half = width // 2
    experts = place_ref.shape[1]
    core = lax.axis_index("local")
    section = lax.axis_index("section")
    node = lax.axis_index("node")
    z, y, x = node // 8, (node // 2) % 4, node % 2
    p = z + core * (y - z)
    q = y + core * (z - y)
    step_p = 8 - 6 * core
    step_q = 2 + 6 * core

    def at_node(dp, dq, dx):
        n = ((p + dp) % RING) * step_p + ((q + dq) % RING) * step_q + (x + dx) % 2
        return {"node": n, "local": core, "section": section}

    p_up, p_down = at_node(1, 0, 0), at_node(3, 0, 0)
    q_up, q_down = at_node(0, 1, 0), at_node(0, 3, 0)
    x_side = at_node(0, 0, 1)
    twin = {"node": node, "local": 1 - core, "section": section}
    after = {"node": node, "local": core, "section": 1 - section}

    def send(src, dst, s, r, to):
        return pltpu.make_async_remote_copy(src_ref=src, dst_ref=dst, send_sem=s, recv_sem=r,
                                            device_id=to, device_id_type=MESH)

    barrier = pltpu.get_barrier_semaphore()
    peers = (p_up, p_down, q_up, q_down, x_side, twin, after)
    for peer in peers:
        pl.semaphore_signal(barrier, inc=1, device_id=peer, device_id_type=MESH)
    pl.semaphore_wait(barrier, len(peers))

    def lanes(c):
        return pl.ds(pl.multiple_of(c * width, width), width)

    lo, hi = pl.ds(0, half), pl.ds(half, half)

    def d_p_up(c):
        return send(tok.at[:, lanes(c)], blocks.at[c, 0, 3], d_s.at[0, c], d_r.at[0, c], p_up)

    def d_p_down(c):
        return send(tok.at[:, lanes(c)], blocks.at[c, 0, 1], d_s.at[1, c], d_r.at[1, c], p_down)

    def d_f_up(c):
        return send(blocks.at[c, 0, 3, :, lo], blocks.at[c, 0, 2, :, lo], d_s.at[2, c], d_r.at[2, c], p_up)

    def d_f_down(c):
        return send(blocks.at[c, 0, 1, :, hi], blocks.at[c, 0, 2, :, hi], d_s.at[3, c], d_r.at[3, c], p_down)

    def d_x(c):
        return send(blocks.at[c, 0], blocks.at[c, 1], d_s.at[4, c], d_r.at[4, c], x_side)

    def d_q_up(c):
        return send(staged.at[c % STAGES, 0], rows.at[c, 3], d_s.at[5, c], d_r.at[5, c], q_up)

    def d_q_down(c):
        return send(staged.at[c % STAGES, 1], rows.at[c, 1], d_s.at[6, c], d_r.at[6, c], q_down)

    def d_t_up(c):
        return send(staged.at[c % STAGES, 2, :, :, :, lo], transit.at[c, 0], d_s.at[7, c], d_r.at[7, c], q_up)

    def d_t_down(c):
        return send(staged.at[c % STAGES, 2, :, :, :, hi], transit.at[c, 1], d_s.at[8, c], d_r.at[8, c], q_down)

    def d_u_up(c):
        return send(transit.at[c, 0], rows.at[c, 2, :, :, :, lo], d_s.at[9, c], d_r.at[9, c], q_up)

    def d_u_down(c):
        return send(transit.at[c, 1], rows.at[c, 2, :, :, :, hi], d_s.at[10, c], d_r.at[10, c], q_down)

    def d_twin(c, k):
        return send(rows.at[c, k], rows_x.at[c, :, k], l_s.at[k, c], l_r.at[k, c], twin)

    def h_twin(k):
        return send(hid.at[k], hid_x.at[:, k], h_s.at[k], h_r.at[k], twin)

    def c_q_up(c):
        return send(rows.at[c, 1], rows_x.at[c, 3], c_s.at[0, c], c_r.at[0, c], q_up)

    def c_q_down(c):
        return send(rows.at[c, 3], rows_x.at[c, 1], c_s.at[1, c], c_r.at[1, c], q_down)

    def c_t_up(c):
        return send(rows.at[c, 2, :, :, :, lo], rows_x.at[c, 0, :, :, :, lo], c_s.at[2, c], c_r.at[2, c], q_up)

    def c_t_down(c):
        return send(rows.at[c, 2, :, :, :, hi], rows_x.at[c, 0, :, :, :, hi], c_s.at[3, c], c_r.at[3, c], q_down)

    def c_u_up(c):
        return send(rows_x.at[c, 0, :, :, :, lo], rows_x.at[c, 2, :, :, :, lo], c_s.at[4, c], c_r.at[4, c], q_up)

    def c_u_down(c):
        return send(rows_x.at[c, 0, :, :, :, hi], rows_x.at[c, 2, :, :, :, hi], c_s.at[5, c], c_r.at[5, c], q_down)

    def c_x(c):
        return send(blocks.at[c, 0], blocks.at[c, 1], c_s.at[6, c], c_r.at[6, c], x_side)

    def c_f_up(c):
        return send(far.at[c, :, lo], far_in.at[c, 0], c_s.at[7, c], c_r.at[7, c], p_up)

    def c_f_down(c):
        return send(far.at[c, :, hi], far_in.at[c, 1], c_s.at[8, c], c_r.at[8, c], p_down)

    def c_p_up(c):
        return send(near.at[c, 0], near_in.at[c, 0], c_s.at[9, c], c_r.at[9, c], p_up)

    def c_p_down(c):
        return send(near.at[c, 1], near_in.at[c, 1], c_s.at[10, c], c_r.at[10, c], p_down)

    def c_out(c):
        return send(done.at[c], out.at[:, lanes(c)], c_s.at[11, c], c_r.at[11, c], after)

    load_g = pltpu.make_async_copy(wg_hbm.at[0, 0], wg, w_sem.at[0])
    load_u = pltpu.make_async_copy(wu_hbm.at[0, 0], wu, w_sem.at[1])
    load_d = pltpu.make_async_copy(
        wd_hbm.at[0, 0, :, pl.ds(pl.multiple_of(core * feats, feats), feats)], wd.at[0], w_sem.at[2])
    give_d = send(wd_hbm.at[0, 0, :, pl.ds(pl.multiple_of((1 - core) * feats, feats), feats)], wd.at[1],
                  wd_s.at[0], wd_r.at[0], twin)

    ids = ids_ref[...]
    home = jnp.zeros_like(ids)
    for e in range(experts):
        home = jnp.where(ids == e, place_ref[0, e], home)
    m_index = lax.broadcasted_iota(jnp.int32, (experts, n_tok), 0)
    chosen = jnp.zeros((experts, n_tok), F32)
    weight = jnp.zeros((experts, n_tok), F32)
    for k in range(ids.shape[0]):
        same = home[k:k + 1, :] == m_index
        chosen = chosen + jnp.where(same, 1.0, 0.0)
        weight = weight + jnp.where(same, gates_ref[k:k + 1, :], 0.0)
    earlier = jnp.where(lax.broadcasted_iota(jnp.int32, (n_tok, n_tok), 0)
                        < lax.broadcasted_iota(jnp.int32, (n_tok, n_tok), 1), 1.0, 0.0).astype(BF)
    count = jnp.dot(chosen.astype(BF), earlier, preferred_element_type=F32)
    aux[0, 0, :experts, :] = jnp.where(chosen > 0.5, count, -1.0)
    aux[0, 0, experts:, :] = weight

    a_up = send(aux.at[0, 0], aux.at[0, 3], aux_s.at[0], aux_r.at[0], p_up)
    a_down = send(aux.at[0, 0], aux.at[0, 1], aux_s.at[1], aux_r.at[1], p_down)
    a_f = send(aux.at[0, 3], aux.at[0, 2], aux_s.at[2], aux_r.at[2], p_up)
    a_x = send(aux.at[0], aux.at[1], aux_s.at[3], aux_r.at[3], x_side)
    a_up.start()
    a_down.start()
    AHEAD = 3
    for c in range(AHEAD):
        d_p_up(c).start()
        d_p_down(c).start()
    load_g.start()
    load_u.start()
    load_d.start()
    give_d.start()

    @pl.loop(0, CHUNKS)
    def _(c):
        blocks[c, 0, 0] = tok[:, lanes(c)]

    acc_g[...] = jnp.zeros_like(acc_g)
    acc_u[...] = jnp.zeros_like(acc_u)
    a_up.wait_recv()
    a_down.wait_recv()
    a_f.start()
    a_f.wait_recv()
    a_x.start()
    slot_index = lax.broadcasted_iota(jnp.int32, (CAP, n_tok), 0).astype(F32)

    def tables(side):
        @pl.loop(0, RING)
        def _(b):
            parts = []
            for k in range(RING):
                m = p * step_p + ((q + k) % RING) * step_q + x
                here = aux[side, b, pl.ds(m, 1), :] == slot_index
                pick[side, b, k * CAP:(k + 1) * CAP, :] = jnp.where(here, 1.0, 0.0).astype(BF)
                parts.append(jnp.where(here, aux[side, b, pl.ds(experts + m, 1), :], 0.0))
            whole = jnp.concatenate(parts, axis=0).T
            top = whole.astype(BF)
            spread[0, side, b] = top
            spread[1, side, b] = (whole - top.astype(F32)).astype(BF)

    tables(0)
    a_x.wait_recv()
    tables(1)
    load_g.wait()
    load_u.wait()

    def accumulate(c):
        own = pl.ds(pl.multiple_of(core * feats + c * width, width), width)
        other = pl.ds(pl.multiple_of((1 - core) * feats + c * width, width), width)

        @pl.loop(0, 2 * RING)
        def _(t):
            k, b = t // 2, (t % 2) * 2
            mine = rows[c, k, pl.ds(b, 2)].reshape(4 * CAP, width)
            theirs = rows_x[c, k, pl.ds(b, 2)].reshape(4 * CAP, width)
            where = pl.ds(pl.multiple_of(t * 4 * CAP, 4 * CAP), 4 * CAP)
            acc_g[where, :] += (jnp.dot(mine, wg[own, :], preferred_element_type=F32)
                                + jnp.dot(theirs, wg[other, :], preferred_element_type=F32))
            acc_u[where, :] += (jnp.dot(mine, wu[own, :], preferred_element_type=F32)
                                + jnp.dot(theirs, wu[other, :], preferred_element_type=F32))

    def within(c):
        return (c >= 0) & (c < CHUNKS)

    @pl.loop(0, CHUNKS + 6)
    def _(i):
        @pl.when(i + AHEAD < CHUNKS)
        def _():
            d_p_up(i + AHEAD).start()
            d_p_down(i + AHEAD).start()

        @pl.when(within(i))
        def _():
            d_p_up(i).wait_recv()
            d_f_up(i).start()
            d_p_down(i).wait_recv()
            d_f_down(i).start()

        @pl.when(within(i - 1))
        def _():
            c = i - 1
            d_f_up(c).wait_recv()
            d_f_down(c).wait_recv()
            d_x(c).start()

        @pl.when(within(i - 2))
        def _():
            c = i - 2

            @pl.when(c >= STAGES)
            def _():
                d_q_up(c - STAGES).wait_send()
                d_q_down(c - STAGES).wait_send()
                d_t_up(c - STAGES).wait_send()
                d_t_down(c - STAGES).wait_send()

            d_x(c).wait_recv()
            for side in range(2):
                for b in range(RING):
                    got = jnp.dot(pick[side, b], blocks[c, side, b], preferred_element_type=F32).astype(BF)
                    rows[c, 0, b, side] = got[:CAP]
                    staged[c % STAGES, 0, b, side] = got[CAP:2 * CAP]
                    staged[c % STAGES, 2, b, side] = got[2 * CAP:3 * CAP]
                    staged[c % STAGES, 1, b, side] = got[3 * CAP:]
            d_t_up(c).start()
            d_t_down(c).start()
            d_q_up(c).start()
            d_q_down(c).start()
            d_twin(c, 0).start()

        @pl.when(within(i - 3))
        def _():
            c = i - 3
            d_t_up(c).wait_recv()
            d_u_up(c).start()
            d_t_down(c).wait_recv()
            d_u_down(c).start()

        @pl.when(within(i - 4))
        def _():
            c = i - 4
            d_q_up(c).wait_recv()
            d_twin(c, 3).start()
            d_q_down(c).wait_recv()
            d_twin(c, 1).start()
            d_u_up(c).wait_recv()
            d_u_down(c).wait_recv()
            d_twin(c, 2).start()

        @pl.when(within(i - 5))
        def _():
            c = i - 5
            for k in range(RING):
                d_twin(c, k).wait_recv()
            accumulate(c)

    pl.semaphore_signal(ready_q, inc=1, device_id=q_up, device_id_type=MESH)
    pl.semaphore_signal(ready_q, inc=1, device_id=q_down, device_id_type=MESH)
    pl.semaphore_signal(ready_x, inc=1, device_id=x_side, device_id_type=MESH)

    for k in range(RING):
        @pl.loop(0, 2)
        def _(t):
            where = pl.ds(pl.multiple_of((2 * k + t) * 4 * CAP, 4 * CAP), 4 * CAP)
            g = acc_g[where, :]
            h = g / (1.0 + jnp.exp(-g)) * acc_u[where, :]
            hid[k, pl.ds(t * 2, 2)] = h.astype(BF).reshape(2, 2, CAP, h.shape[-1])
        h_twin(k).start()

    @pl.loop(0, CHUNKS)
    def _(c):
        for copy in (d_p_up, d_p_down, d_f_up, d_f_down, d_x, d_u_up, d_u_down):
            copy(c).wait_send()
        for k in range(RING):
            d_twin(c, k).wait_send()

    @pl.loop(CHUNKS - STAGES, CHUNKS)
    def _(c):
        for copy in (d_q_up, d_q_down, d_t_up, d_t_down):
            copy(c).wait_send()
    for copy in (a_up, a_down, a_f, a_x):
        copy.wait_send()
    load_d.wait()
    give_d.wait()
    for k in range(RING):
        h_twin(k).wait_recv()
    pl.semaphore_wait(ready_q, 2)
    pl.semaphore_wait(ready_x, 1)

    def spread_out(c, side, b):
        got = jnp.concatenate(
            [rows[c, 0, b, side], rows_x[c, 1, b, side], rows_x[c, 2, b, side], rows_x[c, 3, b, side]], axis=0)
        return (jnp.dot(spread[0, side, b], got, preferred_element_type=F32)
                + jnp.dot(spread[1, side, b], got, preferred_element_type=F32))

    @pl.loop(0, CHUNKS + 5)
    def _(i):
        @pl.when(within(i))
        def _():
            c = i

            @pl.loop(0, 2 * RING)
            def _(t):
                k, b = t // 2, (t % 2) * 2
                mine = hid[k, pl.ds(b, 2)].reshape(4 * CAP, hid.shape[-1])
                theirs = hid_x[k, pl.ds(b, 2)].reshape(4 * CAP, hid.shape[-1])
                made = (jnp.dot(mine, wd[0, :, lanes(c)], preferred_element_type=F32)
                        + jnp.dot(theirs, wd[1, :, lanes(c)], preferred_element_type=F32))
                rows[c, k, pl.ds(b, 2)] = made.astype(BF).reshape(2, 2, CAP, width)

            c_t_up(c).start()
            c_t_down(c).start()
            c_q_up(c).start()
            c_q_down(c).start()

        @pl.when(within(i - 1))
        def _():
            c = i - 1
            c_t_up(c).wait_recv()
            c_u_up(c).start()
            c_t_down(c).wait_recv()
            c_u_down(c).start()

        @pl.when(within(i - 2))
        def _():
            c = i - 2
            c_q_up(c).wait_recv()
            c_q_down(c).wait_recv()
            c_u_up(c).wait_recv()
            c_u_down(c).wait_recv()
            for b in range(RING):
                blocks[c, 0, b] = spread_out(c, 1, b).astype(BF)
            c_x(c).start()

        @pl.when(within(i - 3))
        def _():
            c = i - 3
            c_x(c).wait_recv()
            far[c] = (spread_out(c, 0, 2) + blocks[c, 1, 2].astype(F32)).astype(BF)
            c_f_up(c).start()
            c_f_down(c).start()
            for place, b in enumerate((0, 1, 3)):
                kept[c % KEEP, place] = spread_out(c, 0, b) + blocks[c, 1, b].astype(F32)

        @pl.when(within(i - 4))
        def _():
            c = i - 4
            c_f_up(c).wait_recv()
            near[c, 0, :, :half] = (kept[c % KEEP, 1, :, :half] + far_in[c, 0].astype(F32)).astype(BF)
            near[c, 0, :, half:] = kept[c % KEEP, 1, :, half:].astype(BF)
            c_p_up(c).start()
            c_f_down(c).wait_recv()
            near[c, 1, :, :half] = kept[c % KEEP, 2, :, :half].astype(BF)
            near[c, 1, :, half:] = (kept[c % KEEP, 2, :, half:] + far_in[c, 1].astype(F32)).astype(BF)
            c_p_down(c).start()

        @pl.when(within(i - 5))
        def _():
            c = i - 5
            c_p_up(c).wait_recv()
            c_p_down(c).wait_recv()
            total = kept[c % KEEP, 0] + near_in[c, 0].astype(F32) + near_in[c, 1].astype(F32)
            done[c] = (total + tok[:, lanes(c)].astype(F32)).astype(BF)
            c_out(c).start()

    for k in range(RING):
        h_twin(k).wait_send()

    @pl.loop(0, CHUNKS)
    def _(c):
        c_out(c).wait_recv()
        for copy in (c_q_up, c_q_down, c_t_up, c_t_down, c_u_up, c_u_down, c_x, c_f_up, c_f_down,
                     c_p_up, c_p_down, c_out):
            copy(c).wait_send()


def body(tokens, expert_ids, gate_weights, expert_node, w_gate, w_up, w_down):
    own = tokens[0]
    n_tok, feats = own.shape
    width = feats // CHUNKS
    hidden = w_gate.shape[3]
    deep = w_gate.shape[2]
    total = 8 * RING * CAP
    vmem = pl.BlockSpec(memory_space=pltpu.VMEM)
    anywhere = pl.BlockSpec(memory_space=pl.ANY)
    dma = pltpu.SemaphoreType.DMA
    held = pltpu.VMEM
    out = pl.pallas_call(
        kernel,
        out_shape=jax.ShapeDtypeStruct((n_tok, feats), BF),
        in_specs=[vmem, vmem, pl.BlockSpec(memory_space=pltpu.SMEM), vmem, anywhere, anywhere, anywhere],
        out_specs=anywhere,
        scratch_shapes=[
            held((CHUNKS, 2, RING, n_tok, width), BF),
            held((2, RING, 2 * expert_node.shape[1], n_tok), F32),
            held((2, RING, RING * CAP, n_tok), BF),
            held((2, 2, RING, n_tok, RING * CAP), BF),
            held((STAGES, 3, RING, 2, CAP, width), BF),
            held((CHUNKS, RING, RING, 2, CAP, width), BF),
            held((CHUNKS, RING, RING, 2, CAP, width), BF),
            held((CHUNKS, 2, RING, 2, CAP, width // 2), BF),
            held((total, hidden), F32),
            held((total, hidden), F32),
            held((deep, hidden), BF),
            held((deep, hidden), BF),
            held((2, hidden, feats), BF),
            held((RING, RING, 2, CAP, hidden), BF),
            held((RING, RING, 2, CAP, hidden), BF),
            held((CHUNKS, n_tok, width), BF),
            held((KEEP, 3, n_tok, width), F32),
            held((CHUNKS, 2, n_tok, width // 2), BF),
            held((CHUNKS, 2, n_tok, width), BF),
            held((CHUNKS, 2, n_tok, width), BF),
            held((CHUNKS, n_tok, width), BF),
            dma((3,)),
            dma((4,)),
            dma((4,)),
            dma((1,)),
            dma((1,)),
            dma((11, CHUNKS)),
            dma((11, CHUNKS)),
            dma((RING, CHUNKS)),
            dma((RING, CHUNKS)),
            dma((RING,)),
            dma((RING,)),
            dma((12, CHUNKS)),
            dma((12, CHUNKS)),
            pltpu.SemaphoreType.REGULAR,
            pltpu.SemaphoreType.REGULAR,
        ],
        compiler_params=pltpu.CompilerParams(
            collective_id=0, has_side_effects=True, vmem_limit_bytes=60 * 1024 * 1024),
        name="expert_layer",
    )(expert_ids[0].T, gate_weights[0].T, expert_node, own, w_gate, w_up, w_down)
    return out[None]


def solution(mesh):
    in_specs = (
        P("section", "node", "local"),
        P("section", "node", None),
        P("section", "node", None),
        P("section", None),
        P("section", "node", None, "local"),
        P("section", "node", None, "local"),
        P("section", "node", "local", None),
    )
    out_specs = P("section", "node", "local")
    return jax.shard_map(body, mesh=mesh, in_specs=in_specs, out_specs=out_specs, check_vma=False)
```

time: 439 us -> 188 us (0.43)
  the two profiles are of different devices: /device:TPU:40 before, /device:TPU:0 now
where the time goes in v1:
time: 188 us
  Pallas kernels  186 us (99%)
    pallas_call x1, Pallas kernels, body(): pl.pallas_call(kernel, out_shape=jax.ShapeDtypeStruct((n_tok, feats), BF)...  186 us

profile of v1, /device:TPU:0, one launch (start us, length us, event | category | flops | bytes accessed | tf_op | source)
XLA Modules:
  0.0 187.7 jit_solution(11416471793214402308)
XLA Ops:
  0.0 185.8 %expert_layer.1 = bf16[128,2048]{1,0:T(8,128)(2,1)} custom-call(s32[8,128]{1,0:T(8,128)} %bitcast.10, f32[8,128]{1,0:T(8,128)} %bitcast.11, s32[1,32]{1,0:T(1,128)} %place_ref.1, bf16[128,2048]{1,0:T(8,128)(2,1)} %bitcast.9, bf16[1,1,4096,512]{3,2,1,0:T(8,128)(2,1)} %wg_hbm.1, bf16[1,1,4096,512]{3,2,1,0:T(8,128)(2,1)} %wu_hbm.1, bf16[1,1,512,4096]{3,2,1,0:T(8,128)(2,1)} %wd_hbm.1), custom_call_target="tpu_custom_call" | custom-call | tf_op jit(solution)/shard_map/expert_layer/pallas_call | solution.py:428
  185.8 1.9 %copy.9 = bf16[1,128,2048]{2,1,0:T(8,128)(2,1)} copy(bf16[1,128,2048]{2,1,0:T(8,128)(2,1)} %bitcast.8) | data formatting | bytes 1048576

commit v2 on v1

v2 whole, which is shorter than its diff:
```python
import jax
import jax.numpy as jnp
from jax import lax
from jax.experimental import pallas as pl
from jax.experimental.pallas import tpu as pltpu
from jax.sharding import PartitionSpec as P

MESH = pl.DeviceIdType.MESH
BF = jnp.bfloat16
F32 = jnp.float32
RING = 4
CAP = 64
CHUNKS = 8
STAGES = 3
LAG = 2
X_AHEAD = 2


def kernel(ids_ref, gates_ref, place_ref, tok, wg_hbm, wu_hbm, wd_hbm, out,
           blocks, aux, pick, spread, first, staged, staged_x, rows, rows_x, acc_g, acc_u, wg, wu, wd, hid, hid_x,
           pair_in, parts,
           w_sem, aux_s, aux_r, wd_s, wd_r, o_s, o_r, d_s, d_r, l_s, l_r, h_s, h_r, c_s, c_r, ready_q):
    n_tok, feats = tok.shape
    width = feats // CHUNKS
    experts = place_ref.shape[1]
    core = lax.axis_index("local")
    section = lax.axis_index("section")
    node = lax.axis_index("node")
    z, y, x = node // 8, (node // 2) % 4, node % 2
    p = z + core * (y - z)
    q = y + core * (z - y)
    step_p = 8 - 6 * core
    step_q = 2 + 6 * core

    def at_node(dp, dq, dx, segment=section):
        n = ((p + dp) % RING) * step_p + ((q + dq) % RING) * step_q + (x + dx) % 2
        return {"node": n, "local": core, "section": segment}

    p_peer = [None] + [at_node(d, 0, 0) for d in range(1, RING)]
    q_peer = [None] + [at_node(0, d, 0) for d in range(1, RING)]
    x_side = at_node(0, 0, 1)
    twin = {"node": node, "local": 1 - core, "section": section}
    over = [at_node(d, 0, 1, 1 - section) for d in range(RING)]

    def send(src, dst, s, r, to):
        return pltpu.make_async_remote_copy(src_ref=src, dst_ref=dst, send_sem=s, recv_sem=r,
                                            device_id=to, device_id_type=MESH)

    barrier = pltpu.get_barrier_semaphore()
    peers = p_peer[1:] + q_peer[1:] + [x_side, twin] + over
    for peer in peers:
        pl.semaphore_signal(barrier, inc=1, device_id=peer, device_id_type=MESH)
    pl.semaphore_wait(barrier, len(peers))

    def lanes(c):
        return pl.ds(pl.multiple_of(c * width, width), width)

    def d_p(c, d):
        return send(tok.at[:, lanes(c)], blocks.at[c, 0, RING - d], d_s.at[d, c], d_r.at[d, c], p_peer[d])

    def d_x_own(c):
        return send(blocks.at[c, 0, 0], blocks.at[c, 1, 0], d_s.at[0, c], d_r.at[0, c], x_side)

    def d_x(c):
        return send(blocks.at[c, 0, pl.ds(1, 3)], blocks.at[c, 1, pl.ds(1, 3)], d_s.at[4, c], d_r.at[4, c], x_side)

    def d_first(d):
        return send(first.at[d - 1], rows.at[:, RING - d, 0, 0], o_s.at[d - 1], o_r.at[d - 1], q_peer[d])

    def d_q(c, d):
        return send(staged.at[c % STAGES, d - 1], rows.at[c, RING - d, pl.ds(1, 3), 0],
                    d_s.at[4 + d, c], d_r.at[4 + d, c], q_peer[d])

    def d_qx(c, d):
        return send(staged_x.at[c % STAGES, d - 1], rows.at[c, RING - d, :, 1],
                    d_s.at[7 + d, c], d_r.at[7 + d, c], q_peer[d])

    def d_twin(c, k):
        return send(rows.at[c, k], rows_x.at[c, :, k], l_s.at[k, c], l_r.at[k, c], twin)

    def h_twin(k):
        return send(hid.at[k], hid_x.at[:, k], h_s.at[k], h_r.at[k], twin)

    def c_q(c, d):
        return send(rows.at[c, d], rows_x.at[c, RING - d], c_s.at[d, c], c_r.at[d, c], q_peer[d])

    def c_x(c):
        return send(blocks.at[c, 0], pair_in.at[c], c_s.at[0, c], c_r.at[0, c], x_side)

    def c_over(c, d):
        return send(blocks.at[c, 1, d], parts.at[c, d], c_s.at[4 + d, c], c_r.at[4 + d, c], over[d])

    load_g = pltpu.make_async_copy(wg_hbm.at[0, 0], wg, w_sem.at[0])
    load_u = pltpu.make_async_copy(wu_hbm.at[0, 0], wu, w_sem.at[1])
    load_d = pltpu.make_async_copy(
        wd_hbm.at[0, 0, :, pl.ds(pl.multiple_of(core * feats, feats), feats)], wd.at[0], w_sem.at[2])
    give_d = send(wd_hbm.at[0, 0, :, pl.ds(pl.multiple_of((1 - core) * feats, feats), feats)], wd.at[1],
                  wd_s.at[0], wd_r.at[0], twin)

    for c in range(CHUNKS):
        for d in (1, 3, 2):
            d_p(c, d).start()

    ids = ids_ref[...]
    home = jnp.zeros_like(ids)
    for e in range(experts):
        home = jnp.where(ids == e, place_ref[0, e], home)
    m_index = lax.broadcasted_iota(jnp.int32, (experts, n_tok), 0)
    chosen = jnp.zeros((experts, n_tok), F32)
    weight = jnp.zeros((experts, n_tok), F32)
    for k in range(ids.shape[0]):
        same = home[k:k + 1, :] == m_index
        chosen = chosen + jnp.where(same, 1.0, 0.0)
        weight = weight + jnp.where(same, gates_ref[k:k + 1, :], 0.0)
    earlier = jnp.where(lax.broadcasted_iota(jnp.int32, (n_tok, n_tok), 0)
                        < lax.broadcasted_iota(jnp.int32, (n_tok, n_tok), 1), 1.0, 0.0).astype(BF)
    count = jnp.dot(chosen.astype(BF), earlier, preferred_element_type=F32)
    aux[0, 0, :experts, :] = jnp.where(chosen > 0.5, count, -1.0)
    aux[0, 0, experts:, :] = weight

    a_p = [None] + [send(aux.at[0, 0], aux.at[0, RING - d], aux_s.at[d], aux_r.at[d], p_peer[d])
                    for d in range(1, RING)]
    a_x = send(aux.at[0], aux.at[1], aux_s.at[0], aux_r.at[0], x_side)
    for d in range(1, RING):
        a_p[d].start()

    slot_index = lax.broadcasted_iota(jnp.int32, (CAP, n_tok), 0).astype(F32)

    def table(side, b):
        parts_of = []
        for k in range(RING):
            m = p * step_p + ((q + k) % RING) * step_q + x
            here = aux[side, b, pl.ds(m, 1), :] == slot_index
            pick[side, b, k * CAP:(k + 1) * CAP, :] = jnp.where(here, 1.0, 0.0).astype(BF)
            parts_of.append(jnp.where(here, aux[side, b, pl.ds(experts + m, 1), :], 0.0))
        whole = jnp.concatenate(parts_of, axis=0).T
        top = whole.astype(BF)
        spread[0, side, b] = top
        spread[1, side, b] = (whole - top.astype(F32)).astype(BF)

    table(0, 0)
    for c in range(CHUNKS):
        mine = tok[:, c * width:(c + 1) * width]
        blocks[c, 0, 0] = mine
        if c < X_AHEAD:
            d_x_own(c).start()
        got = jnp.dot(pick[0, 0], mine, preferred_element_type=F32).astype(BF)
        rows[c, 0, 0, 0] = got[:CAP]
        for d in range(1, RING):
            first[d - 1, c] = got[d * CAP:(d + 1) * CAP]
    for d in (2, 1, 3):
        d_first(d).start()
    load_g.start()
    load_u.start()
    load_d.start()
    give_d.start()
    for d in range(1, RING):
        a_p[d].wait_recv()
    a_x.start()

    @pl.loop(1, RING)
    def _(b):
        table(0, b)

    acc_g[...] = jnp.zeros_like(acc_g)
    acc_u[...] = jnp.zeros_like(acc_u)

    def accumulate(c):
        own = pl.ds(pl.multiple_of(core * feats + c * width, width), width)
        other = pl.ds(pl.multiple_of((1 - core) * feats + c * width, width), width)

        @pl.loop(0, 2 * RING)
        def _(t):
            k, b = t // 2, (t % 2) * 2
            mine = rows[c, k, pl.ds(b, 2)].reshape(4 * CAP, width)
            theirs = rows_x[c, k, pl.ds(b, 2)].reshape(4 * CAP, width)
            where = pl.ds(pl.multiple_of(t * 4 * CAP, 4 * CAP), 4 * CAP)
            acc_g[where, :] += (jnp.dot(mine, wg[own, :], preferred_element_type=F32)
                                + jnp.dot(theirs, wg[other, :], preferred_element_type=F32))
            acc_u[where, :] += (jnp.dot(mine, wu[own, :], preferred_element_type=F32)
                                + jnp.dot(theirs, wu[other, :], preferred_element_type=F32))

    def within(c):
        return (c >= 0) & (c < CHUNKS)

    @pl.loop(0, CHUNKS + LAG + 2)
    def _(i):
        @pl.when(within(i))
        def _():
            c = i
            for d in (1, 3, 2):
                d_p(c, d).wait_recv()
            d_x(c).start()

            @pl.when(c + X_AHEAD < CHUNKS)
            def _():
                d_x_own(c + X_AHEAD).start()

            @pl.when(c >= STAGES)
            def _():
                for d in range(1, RING):
                    d_q(c - STAGES, d).wait_send()

            for b in range(1, RING):
                got = jnp.dot(pick[0, b], blocks[c, 0, b], preferred_element_type=F32).astype(BF)
                rows[c, 0, b, 0] = got[:CAP]
                for d in range(1, RING):
                    staged[c % STAGES, d - 1, b - 1] = got[d * CAP:(d + 1) * CAP]
            for d in (2, 1, 3):
                d_q(c, d).start()

        @pl.when(i == LAG - 1)
        def _():
            a_x.wait_recv()

            @pl.loop(0, RING)
            def _(b):
                table(1, b)

        @pl.when(within(i - LAG))
        def _():
            c = i - LAG
            d_x_own(c).wait_recv()
            d_x(c).wait_recv()

            @pl.when(c >= STAGES)
            def _():
                for d in range(1, RING):
                    d_qx(c - STAGES, d).wait_send()

            for b in range(RING):
                got = jnp.dot(pick[1, b], blocks[c, 1, b], preferred_element_type=F32).astype(BF)
                rows[c, 0, b, 1] = got[:CAP]
                for d in range(1, RING):
                    staged_x[c % STAGES, d - 1, b] = got[d * CAP:(d + 1) * CAP]
            for d in (2, 1, 3):
                d_qx(c, d).start()
            d_twin(c, 0).start()

        @pl.when(within(i - LAG - 1))
        def _():
            c = i - LAG - 1

            @pl.when(c == 0)
            def _():
                for d in range(1, RING):
                    d_first(d).wait_recv()
            for d in range(1, RING):
                d_q(c, d).wait_recv()
                d_qx(c, d).wait_recv()
                d_twin(c, RING - d).start()

        @pl.when(within(i - LAG - 2))
        def _():
            c = i - LAG - 2

            @pl.when(c == 0)
            def _():
                load_g.wait()
                load_u.wait()
            for k in range(RING):
                d_twin(c, k).wait_recv()
            accumulate(c)

    for d in range(1, RING):
        pl.semaphore_signal(ready_q, inc=1, device_id=q_peer[d], device_id_type=MESH)

    for k in range(RING):
        @pl.loop(0, 2)
        def _(t):
            where = pl.ds(pl.multiple_of((2 * k + t) * 4 * CAP, 4 * CAP), 4 * CAP)
            g = acc_g[where, :]
            h = g / (1.0 + jnp.exp(-g)) * acc_u[where, :]
            hid[k, pl.ds(t * 2, 2)] = h.astype(BF).reshape(2, 2, CAP, h.shape[-1])
        h_twin(k).start()

    @pl.loop(0, CHUNKS)
    def _(c):
        for d in range(1, RING):
            d_p(c, d).wait_send()
        d_x_own(c).wait_send()
        d_x(c).wait_send()
        for k in range(RING):
            d_twin(c, k).wait_send()

    @pl.loop(CHUNKS - STAGES, CHUNKS)
    def _(c):
        for d in range(1, RING):
            d_q(c, d).wait_send()
            d_qx(c, d).wait_send()
    for d in range(1, RING):
        a_p[d].wait_send()
        d_first(d).wait_send()
    a_x.wait_send()
    load_d.wait()
    give_d.wait()
    for k in range(RING):
        h_twin(k).wait_recv()
    pl.semaphore_wait(ready_q, RING - 1)

    def spread_out(c, side, b):
        got = jnp.concatenate(
            [rows[c, 0, b, side], rows_x[c, 1, b, side], rows_x[c, 2, b, side], rows_x[c, 3, b, side]], axis=0)
        return (jnp.dot(spread[0, side, b], got, preferred_element_type=F32)
                + jnp.dot(spread[1, side, b], got, preferred_element_type=F32))

    @pl.loop(0, CHUNKS + 3)
    def _(i):
        @pl.when(within(i))
        def _():
            c = i

            @pl.loop(0, 2 * RING)
            def _(t):
                k, b = t // 2, (t % 2) * 2
                mine = hid[k, pl.ds(b, 2)].reshape(4 * CAP, hid.shape[-1])
                theirs = hid_x[k, pl.ds(b, 2)].reshape(4 * CAP, hid.shape[-1])
                made = (jnp.dot(mine, wd[0, :, lanes(c)], preferred_element_type=F32)
                        + jnp.dot(theirs, wd[1, :, lanes(c)], preferred_element_type=F32))
                rows[c, k, pl.ds(b, 2)] = made.astype(BF).reshape(2, 2, CAP, width)

            for d in (2, 1, 3):
                c_q(c, d).start()

        @pl.when(within(i - 1))
        def _():
            c = i - 1
            for d in range(1, RING):
                c_q(c, d).wait_recv()
            for b in range(RING):
                blocks[c, 0, b] = spread_out(c, 0, b).astype(BF)
            c_x(c).start()

        @pl.when(within(i - 2))
        def _():
            c = i - 2
            c_x(c).wait_recv()
            for b in (2, 1, 3, 0):
                total = spread_out(c, 1, b) + pair_in[c, b].astype(F32)
                if b == 0:
                    total = total + blocks[c, 1, 0].astype(F32)
                blocks[c, 1, b] = total.astype(BF)
                c_over(c, b).start()

        @pl.when(within(i - 3))
        def _():
            c = i - 3
            for d in range(RING):
                c_over(c, d).wait_recv()
            total = parts[c, 0].astype(F32) + parts[c, 1].astype(F32)
            total = total + parts[c, 2].astype(F32) + parts[c, 3].astype(F32)
            out[:, lanes(c)] = total.astype(BF)

    for k in range(RING):
        h_twin(k).wait_send()

    @pl.loop(0, CHUNKS)
    def _(c):
        for d in range(1, RING):
            c_q(c, d).wait_send()
        c_x(c).wait_send()
        for d in range(RING):
            c_over(c, d).wait_send()


def body(tokens, expert_ids, gate_weights, expert_node, w_gate, w_up, w_down):
    own = tokens[0]
    n_tok, feats = own.shape
    width = feats // CHUNKS
    hidden = w_gate.shape[3]
    deep = w_gate.shape[2]
    total = 8 * RING * CAP
    vmem = pl.BlockSpec(memory_space=pltpu.VMEM)
    anywhere = pl.BlockSpec(memory_space=pl.ANY)
    dma = pltpu.SemaphoreType.DMA
    held = pltpu.VMEM
    out = pl.pallas_call(
        kernel,
        out_shape=jax.ShapeDtypeStruct((n_tok, feats), BF),
        in_specs=[vmem, vmem, pl.BlockSpec(memory_space=pltpu.SMEM), vmem, anywhere, anywhere, anywhere],
        out_specs=vmem,
        scratch_shapes=[
            held((CHUNKS, 2, RING, n_tok, width), BF),
            held((2, RING, 2 * expert_node.shape[1], n_tok), F32),
            held((2, RING, RING * CAP, n_tok), BF),
            held((2, 2, RING, n_tok, RING * CAP), BF),
            held((RING - 1, CHUNKS, CAP, width), BF),
            held((STAGES, RING - 1, RING - 1, CAP, width), BF),
            held((STAGES, RING - 1, RING, CAP, width), BF),
            held((CHUNKS, RING, RING, 2, CAP, width), BF),
            held((CHUNKS, RING, RING, 2, CAP, width), BF),
            held((total, hidden), F32),
            held((total, hidden), F32),
            held((deep, hidden), BF),
            held((deep, hidden), BF),
            held((2, hidden, feats), BF),
            held((RING, RING, 2, CAP, hidden), BF),
            held((RING, RING, 2, CAP, hidden), BF),
            held((CHUNKS, RING, n_tok, width), BF),
            held((CHUNKS, RING, n_tok, width), BF),
            dma((3,)),
            dma((RING,)),
            dma((RING,)),
            dma((1,)),
            dma((1,)),
            dma((RING - 1,)),
            dma((RING - 1,)),
            dma((11, CHUNKS)),
            dma((11, CHUNKS)),
            dma((RING, CHUNKS)),
            dma((RING, CHUNKS)),
            dma((RING,)),
            dma((RING,)),
            dma((8, CHUNKS)),
            dma((8, CHUNKS)),
            pltpu.SemaphoreType.REGULAR,
        ],
        compiler_params=pltpu.CompilerParams(
            collective_id=0, has_side_effects=True, vmem_limit_bytes=60 * 1024 * 1024),
        name="expert_layer",
    )(expert_ids[0].T, gate_weights[0].T, expert_node, own, w_gate, w_up, w_down)
    return out[None]


def solution(mesh):
    in_specs = (
        P("section", "node", "local"),
        P("section", "node", None),
        P("section", "node", None),
        P("section", None),
        P("section", "node", None, "local"),
        P("section", "node", None, "local"),
        P("section", "node", "local", None),
    )
    out_specs = P("section", "node", "local")
    return jax.shard_map(body, mesh=mesh, in_specs=in_specs, out_specs=out_specs, check_vma=False)
```

time: 188 us -> 175 us (0.931)
  Pallas kernels: 186 us -> 173 us
    pallas_call x1, Pallas kernels: 186 us -> 173 us  [body(): pl.pallas_call(kernel, out_shape=jax.ShapeDtypeStruct((n_tok, feats), BF)...]
where the time goes in v2:
time: 175 us
  Pallas kernels  173 us (99%)
  local copies, waits for them, and re-layouts  1.88 us (1%)
    pallas_call x1, Pallas kernels, body(): pl.pallas_call(kernel, out_shape=jax.ShapeDtypeStruct((n_tok, feats), BF)...  173 us

profile of v2, /device:TPU:0, one launch (start us, length us, event | category | flops | bytes accessed | tf_op | source)
XLA Modules:
  0.0 174.9 jit_solution(13765513269550229176)
XLA Ops:
  0.0 173.0 %expert_layer.1 = bf16[128,2048]{1,0:T(8,128)(2,1)} custom-call(s32[8,128]{1,0:T(8,128)} %bitcast.10, f32[8,128]{1,0:T(8,128)} %bitcast.11, s32[1,32]{1,0:T(1,128)} %place_ref.1, bf16[128,2048]{1,0:T(8,128)(2,1)} %bitcast.9, bf16[1,1,4096,512]{3,2,1,0:T(8,128)(2,1)} %wg_hbm.1, bf16[1,1,4096,512]{3,2,1,0:T(8,128)(2,1)} %wu_hbm.1, bf16[1,1,512,4096]{3,2,1,0:T(8,128)(2,1)} %wd_hbm.1), custom_call_target="tpu_custom_call" | custom-call | tf_op jit(solution)/shard_map/expert_layer/pallas_call | solution.py:377
  173.0 1.9 %copy.9 = bf16[1,128,2048]{2,1,0:T(8,128)(2,1)} copy(bf16[1,128,2048]{2,1,0:T(8,128)(2,1)} %bitcast.8) | data formatting | bytes 1048576

commit v3 on v2

v3 whole, which is shorter than its diff:
```python
import jax
import jax.numpy as jnp
from jax import lax
from jax.experimental import pallas as pl
from jax.experimental.pallas import tpu as pltpu
from jax.sharding import PartitionSpec as P

MESH = pl.DeviceIdType.MESH
BF = jnp.bfloat16
F32 = jnp.float32
RING = 4
CAP = 64
CHUNKS = 8
STAGES = 3
LAG = 2
SHARE = 1
ADD = 2
P_AHEAD = 2
X_AHEAD = 2


def kernel(ids_ref, gates_ref, place_ref, tok, wg_hbm, wu_hbm, wd_hbm, out,
           blocks, aux, pick, spread, first, staged, staged_x, rows, rows_x, acc_g, acc_u, wg, wu, wd, hid, hid_x,
           pair_in, parts,
           w_sem, aux_s, aux_r, wd_s, wd_r, o_s, o_r, d_s, d_r, l_s, l_r, h_s, h_r, c_s, c_r, x_s, x_r, ready_q):
    n_tok, feats = tok.shape
    width = feats // CHUNKS
    experts = place_ref.shape[1]
    core = lax.axis_index("local")
    section = lax.axis_index("section")
    node = lax.axis_index("node")
    z, y, x = node // 8, (node // 2) % 4, node % 2
    p = z + core * (y - z)
    q = y + core * (z - y)
    step_p = 8 - 6 * core
    step_q = 2 + 6 * core

    def at_node(dp, dq, dx, segment=section):
        n = ((p + dp) % RING) * step_p + ((q + dq) % RING) * step_q + (x + dx) % 2
        return {"node": n, "local": core, "section": segment}

    p_peer = [None] + [at_node(d, 0, 0) for d in range(1, RING)]
    q_peer = [None] + [at_node(0, d, 0) for d in range(1, RING)]
    x_side = at_node(0, 0, 1)
    twin = {"node": node, "local": 1 - core, "section": section}
    over = [at_node(d, 0, 1, 1 - section) for d in range(RING)]

    def send(src, dst, s, r, to):
        return pltpu.make_async_remote_copy(src_ref=src, dst_ref=dst, send_sem=s, recv_sem=r,
                                            device_id=to, device_id_type=MESH)

    barrier = pltpu.get_barrier_semaphore()
    peers = p_peer[1:] + q_peer[1:] + [x_side, twin] + over
    for peer in peers:
        pl.semaphore_signal(barrier, inc=1, device_id=peer, device_id_type=MESH)
    pl.semaphore_wait(barrier, len(peers))

    def lanes(c):
        return pl.ds(pl.multiple_of(c * width, width), width)

    def d_p(c, d):
        return send(tok.at[:, lanes(c)], blocks.at[c, 0, RING - d], d_s.at[d, c], d_r.at[d, c], p_peer[d])

    def d_x_own(c):
        return send(blocks.at[c, 0, 0], blocks.at[c, 1, 0], d_s.at[0, c], d_r.at[0, c], x_side)

    def d_x(c):
        return send(blocks.at[c, 0, pl.ds(1, 3)], blocks.at[c, 1, pl.ds(1, 3)], d_s.at[4, c], d_r.at[4, c], x_side)

    def d_first(d):
        return send(first.at[d - 1], rows.at[:, RING - d, 0, 0], o_s.at[d - 1], o_r.at[d - 1], q_peer[d])

    def d_q(c, d):
        return send(staged.at[c % STAGES, d - 1], rows.at[c, RING - d, pl.ds(1, 3), 0],
                    d_s.at[4 + d, c], d_r.at[4 + d, c], q_peer[d])

    def d_qx(c, d):
        return send(staged_x.at[c % STAGES, d - 1], rows.at[c, RING - d, :, 1],
                    d_s.at[7 + d, c], d_r.at[7 + d, c], q_peer[d])

    def d_twin(c, side, k):
        return send(rows.at[c, k, :, side], rows_x.at[c, :, k, side], l_s.at[side, k, c], l_r.at[side, k, c], twin)

    def h_twin(side, k):
        return send(hid.at[k, :, side], hid_x.at[:, k, side], h_s.at[side, k], h_r.at[side, k], twin)

    def c_q(c, side, d):
        return send(rows.at[c, d, :, side], rows_x.at[c, RING - d, :, side],
                    c_s.at[side, d - 1, c], c_r.at[side, d - 1, c], q_peer[d])

    def c_x(c):
        return send(blocks.at[c, 0], pair_in.at[c], x_s.at[RING, c], x_r.at[RING, c], x_side)

    def c_over(c, d):
        return send(blocks.at[c, 1, d], parts.at[c, d], x_s.at[d, c], x_r.at[d, c], over[d])

    load_g = pltpu.make_async_copy(wg_hbm.at[0, 0], wg, w_sem.at[0])
    load_u = pltpu.make_async_copy(wu_hbm.at[0, 0], wu, w_sem.at[1])
    load_d = pltpu.make_async_copy(
        wd_hbm.at[0, 0, :, pl.ds(pl.multiple_of(core * feats, feats), feats)], wd.at[0], w_sem.at[2])
    give_d = send(wd_hbm.at[0, 0, :, pl.ds(pl.multiple_of((1 - core) * feats, feats), feats)], wd.at[1],
                  wd_s.at[0], wd_r.at[0], twin)

    for c in range(P_AHEAD):
        for d in (1, 3, 2):
            d_p(c, d).start()

    ids = ids_ref[...]
    home = jnp.zeros_like(ids)
    for e in range(experts):
        home = jnp.where(ids == e, place_ref[0, e], home)
    m_index = lax.broadcasted_iota(jnp.int32, (experts, n_tok), 0)
    chosen = jnp.zeros((experts, n_tok), F32)
    weight = jnp.zeros((experts, n_tok), F32)
    for k in range(ids.shape[0]):
        same = home[k:k + 1, :] == m_index
        chosen = chosen + jnp.where(same, 1.0, 0.0)
        weight = weight + jnp.where(same, gates_ref[k:k + 1, :], 0.0)
    earlier = jnp.where(lax.broadcasted_iota(jnp.int32, (n_tok, n_tok), 0)
                        < lax.broadcasted_iota(jnp.int32, (n_tok, n_tok), 1), 1.0, 0.0).astype(BF)
    count = jnp.dot(chosen.astype(BF), earlier, preferred_element_type=F32)
    aux[0, 0, :experts, :] = jnp.where(chosen > 0.5, count, -1.0)
    aux[0, 0, experts:, :] = weight

    a_p = [None] + [send(aux.at[0, 0], aux.at[0, RING - d], aux_s.at[d], aux_r.at[d], p_peer[d])
                    for d in range(1, RING)]
    a_x = send(aux.at[0], aux.at[1], aux_s.at[0], aux_r.at[0], x_side)
    for d in range(1, RING):
        a_p[d].start()

    slot_index = lax.broadcasted_iota(jnp.int32, (CAP, n_tok), 0).astype(F32)

    def table(side, b):
        parts_of = []
        for k in range(RING):
            m = p * step_p + ((q + k) % RING) * step_q + x
            here = aux[side, b, pl.ds(m, 1), :] == slot_index
            pick[side, b, k * CAP:(k + 1) * CAP, :] = jnp.where(here, 1.0, 0.0).astype(BF)
            parts_of.append(jnp.where(here, aux[side, b, pl.ds(experts + m, 1), :], 0.0))
        whole = jnp.concatenate(parts_of, axis=0).T
        top = whole.astype(BF)
        spread[0, side, b] = top
        spread[1, side, b] = (whole - top.astype(F32)).astype(BF)

    table(0, 0)
    for c in range(CHUNKS):
        mine = tok[:, c * width:(c + 1) * width]
        blocks[c, 0, 0] = mine
        if c < X_AHEAD:
            d_x_own(c).start()
        got = jnp.dot(pick[0, 0], mine, preferred_element_type=F32).astype(BF)
        rows[c, 0, 0, 0] = got[:CAP]
        for d in range(1, RING):
            first[d - 1, c] = got[d * CAP:(d + 1) * CAP]
    for d in (2, 1, 3):
        d_first(d).start()
    load_g.start()
    load_u.start()
    load_d.start()
    give_d.start()
    for d in range(1, RING):
        a_p[d].wait_recv()
    a_x.start()

    @pl.loop(1, RING)
    def _(b):
        table(0, b)

    acc_g[...] = jnp.zeros_like(acc_g)
    acc_u[...] = jnp.zeros_like(acc_u)

    def accumulate(c, side):
        own = pl.ds(pl.multiple_of(core * feats + c * width, width), width)
        other = pl.ds(pl.multiple_of((1 - core) * feats + c * width, width), width)

        @pl.loop(0, RING)
        def _(k):
            mine = rows[c, k, :, side].reshape(RING * CAP, width)
            theirs = rows_x[c, k, :, side].reshape(RING * CAP, width)
            acc_g[side, k] += (jnp.dot(mine, wg[own, :], preferred_element_type=F32)
                               + jnp.dot(theirs, wg[other, :], preferred_element_type=F32))
            acc_u[side, k] += (jnp.dot(mine, wu[own, :], preferred_element_type=F32)
                               + jnp.dot(theirs, wu[other, :], preferred_element_type=F32))

    def activate(side):
        for d in range(1, RING):
            pl.semaphore_signal(ready_q.at[side], inc=1, device_id=q_peer[d], device_id_type=MESH)

        for k in range(RING):
            g = acc_g[side, k]
            h = g / (1.0 + jnp.exp(-g)) * acc_u[side, k]
            hid[k, :, side] = h.astype(BF).reshape(RING, CAP, h.shape[-1])
            h_twin(side, k).start()

    def project(c, side):
        @pl.loop(0, RING)
        def _(k):
            mine = hid[k, :, side].reshape(RING * CAP, hid.shape[-1])
            theirs = hid_x[k, :, side].reshape(RING * CAP, hid.shape[-1])
            made = (jnp.dot(mine, wd[0, :, lanes(c)], preferred_element_type=F32)
                    + jnp.dot(theirs, wd[1, :, lanes(c)], preferred_element_type=F32))
            rows[c, k, :, side] = made.astype(BF).reshape(RING, CAP, width)

        for d in (2, 1, 3):
            c_q(c, side, d).start()

    def spread_out(c, side, b):
        got = jnp.concatenate(
            [rows[c, 0, b, side], rows_x[c, 1, b, side], rows_x[c, 2, b, side], rows_x[c, 3, b, side]], axis=0)
        return (jnp.dot(spread[0, side, b], got, preferred_element_type=F32)
                + jnp.dot(spread[1, side, b], got, preferred_element_type=F32))

    def stage(c, run):
        @pl.when((c >= 0) & (c < CHUNKS))
        def _():
            run(c)

    def gather_own(c):
        @pl.when(c + P_AHEAD < CHUNKS)
        def _():
            for d in (1, 3, 2):
                d_p(c + P_AHEAD, d).start()
        for d in (1, 3, 2):
            d_p(c, d).wait_recv()
        d_x(c).start()

        @pl.when(c + X_AHEAD < CHUNKS)
        def _():
            d_x_own(c + X_AHEAD).start()

        @pl.when(c >= STAGES)
        def _():
            for d in range(1, RING):
                d_q(c - STAGES, d).wait_send()

        for b in range(1, RING):
            got = jnp.dot(pick[0, b], blocks[c, 0, b], preferred_element_type=F32).astype(BF)
            rows[c, 0, b, 0] = got[:CAP]
            for d in range(1, RING):
                staged[c % STAGES, d - 1, b - 1] = got[d * CAP:(d + 1) * CAP]
        for d in (2, 1, 3):
            d_q(c, d).start()
        d_twin(c, 0, 0).start()

    def gather_other(c):
        @pl.when(c == 0)
        def _():
            a_x.wait_recv()

            @pl.loop(0, RING)
            def _(b):
                table(1, b)

        d_x_own(c).wait_recv()
        d_x(c).wait_recv()

        @pl.when(c >= STAGES)
        def _():
            for d in range(1, RING):
                d_qx(c - STAGES, d).wait_send()

        for b in range(RING):
            got = jnp.dot(pick[1, b], blocks[c, 1, b], preferred_element_type=F32).astype(BF)
            rows[c, 0, b, 1] = got[:CAP]
            for d in range(1, RING):
                staged_x[c % STAGES, d - 1, b] = got[d * CAP:(d + 1) * CAP]
        for d in (2, 1, 3):
            d_qx(c, d).start()
        d_twin(c, 1, 0).start()

    def share_own(c):
        @pl.when(c == 0)
        def _():
            for d in range(1, RING):
                d_first(d).wait_recv()
        for d in range(1, RING):
            d_q(c, d).wait_recv()
            d_twin(c, 0, RING - d).start()

    def share_other(c):
        for d in range(1, RING):
            d_qx(c, d).wait_recv()
            d_twin(c, 1, RING - d).start()

    def multiply_own(c):
        @pl.when(c == 0)
        def _():
            load_g.wait()
            load_u.wait()
        for k in range(RING):
            d_twin(c, 0, k).wait_recv()
        accumulate(c, 0)

        @pl.when(c == CHUNKS - 1)
        def _():
            activate(0)

    def multiply_other(c):
        for k in range(RING):
            d_twin(c, 1, k).wait_recv()
        accumulate(c, 1)

        @pl.when(c == CHUNKS - 1)
        def _():
            activate(1)

    def project_own(c):
        @pl.when(c == 0)
        def _():
            @pl.loop(0, CHUNKS)
            def _(e):
                for d in range(1, RING):
                    d_p(e, d).wait_send()
                d_x_own(e).wait_send()
                d_x(e).wait_send()
                for k in range(RING):
                    d_twin(e, 0, k).wait_send()
            load_d.wait()
            give_d.wait()
            for k in range(RING):
                h_twin(0, k).wait_recv()
            pl.semaphore_wait(ready_q.at[0], RING - 1)
        project(c, 0)

    def project_other(c):
        @pl.when(c == 0)
        def _():
            @pl.loop(0, CHUNKS)
            def _(e):
                for k in range(RING):
                    d_twin(e, 1, k).wait_send()
            for k in range(RING):
                h_twin(1, k).wait_recv()
            pl.semaphore_wait(ready_q.at[1], RING - 1)
        project(c, 1)

    def add_own(c):
        for d in range(1, RING):
            c_q(c, 0, d).wait_recv()
        for b in range(RING):
            blocks[c, 0, b] = spread_out(c, 0, b).astype(BF)
        c_x(c).start()

    def add_other(c):
        for d in range(1, RING):
            c_q(c, 1, d).wait_recv()
        c_x(c).wait_recv()
        for b in (2, 1, 3, 0):
            total = spread_out(c, 1, b) + pair_in[c, b].astype(F32)
            if b == 0:
                total = total + blocks[c, 1, 0].astype(F32)
            blocks[c, 1, b] = total.astype(BF)
            c_over(c, b).start()

    def finish(c):
        for d in range(RING):
            c_over(c, d).wait_recv()
        total = parts[c, 0].astype(F32) + parts[c, 1].astype(F32)
        total = total + parts[c, 2].astype(F32) + parts[c, 3].astype(F32)
        out[:, lanes(c)] = total.astype(BF)

    @pl.loop(0, 2 * CHUNKS + SHARE + ADD + LAG + 2)
    def _(i):
        j = i - CHUNKS - SHARE - 1
        stage(i, gather_own)
        stage(i - LAG, gather_other)
        stage(j, project_own)
        stage(j - LAG, project_other)
        stage(i - SHARE, share_own)
        stage(i - SHARE - LAG, share_other)
        stage(i - SHARE - 1, multiply_own)
        stage(i - SHARE - LAG - 1, multiply_other)
        stage(j - ADD, add_own)
        stage(j - ADD - LAG, add_other)
        stage(j - ADD - LAG - 1, finish)

    @pl.loop(CHUNKS - STAGES, CHUNKS)
    def _(c):
        for d in range(1, RING):
            d_q(c, d).wait_send()
            d_qx(c, d).wait_send()
    for d in range(1, RING):
        a_p[d].wait_send()
        d_first(d).wait_send()
    a_x.wait_send()
    for side in range(2):
        for k in range(RING):
            h_twin(side, k).wait_send()

    @pl.loop(0, CHUNKS)
    def _(c):
        for d in range(1, RING):
            c_q(c, 0, d).wait_send()
            c_q(c, 1, d).wait_send()
        c_x(c).wait_send()
        for d in range(RING):
            c_over(c, d).wait_send()


def body(tokens, expert_ids, gate_weights, expert_node, w_gate, w_up, w_down):
    own = tokens[0]
    n_tok, feats = own.shape
    width = feats // CHUNKS
    hidden = w_gate.shape[3]
    deep = w_gate.shape[2]
    reach = (2, RING, RING * CAP, hidden)
    vmem = pl.BlockSpec(memory_space=pltpu.VMEM)
    anywhere = pl.BlockSpec(memory_space=pl.ANY)
    dma = pltpu.SemaphoreType.DMA
    held = pltpu.VMEM
    out = pl.pallas_call(
        kernel,
        out_shape=jax.ShapeDtypeStruct((n_tok, feats), BF),
        in_specs=[vmem, vmem, pl.BlockSpec(memory_space=pltpu.SMEM), vmem, anywhere, anywhere, anywhere],
        out_specs=vmem,
        scratch_shapes=[
            held((CHUNKS, 2, RING, n_tok, width), BF),
            held((2, RING, 2 * expert_node.shape[1], n_tok), F32),
            held((2, RING, RING * CAP, n_tok), BF),
            held((2, 2, RING, n_tok, RING * CAP), BF),
            held((RING - 1, CHUNKS, CAP, width), BF),
            held((STAGES, RING - 1, RING - 1, CAP, width), BF),
            held((STAGES, RING - 1, RING, CAP, width), BF),
            held((CHUNKS, RING, RING, 2, CAP, width), BF),
            held((CHUNKS, RING, RING, 2, CAP, width), BF),
            held(reach, F32),
            held(reach, F32),
            held((deep, hidden), BF),
            held((deep, hidden), BF),
            held((2, hidden, feats), BF),
            held((RING, RING, 2, CAP, hidden), BF),
            held((RING, RING, 2, CAP, hidden), BF),
            held((CHUNKS, RING, n_tok, width), BF),
            held((CHUNKS, RING, n_tok, width), BF),
            dma((3,)),
            dma((RING,)),
            dma((RING,)),
            dma((1,)),
            dma((1,)),
            dma((RING - 1,)),
            dma((RING - 1,)),
            dma((11, CHUNKS)),
            dma((11, CHUNKS)),
            dma((2, RING, CHUNKS)),
            dma((2, RING, CHUNKS)),
            dma((2, RING)),
            dma((2, RING)),
            dma((2, RING - 1, CHUNKS)),
            dma((2, RING - 1, CHUNKS)),
            dma((RING + 1, CHUNKS)),
            dma((RING + 1, CHUNKS)),
            pltpu.SemaphoreType.REGULAR((2,)),
        ],
        compiler_params=pltpu.CompilerParams(
            collective_id=0, has_side_effects=True, vmem_limit_bytes=60 * 1024 * 1024),
        name="expert_layer",
    )(expert_ids[0].T, gate_weights[0].T, expert_node, own, w_gate, w_up, w_down)
    return out[None]


def solution(mesh):
    in_specs = (
        P("section", "node", "local"),
        P("section", "node", None),
        P("section", "node", None),
        P("section", None),
        P("section", "node", None, "local"),
        P("section", "node", None, "local"),
        P("section", "node", "local", None),
    )
    out_specs = P("section", "node", "local")
    return jax.shard_map(body, mesh=mesh, in_specs=in_specs, out_specs=out_specs, check_vma=False)
```

time: 175 us -> 153 us (0.87)
  Pallas kernels: 173 us -> 150 us
    pallas_call x1, Pallas kernels: 173 us -> 150 us  [body(): pl.pallas_call(kernel, out_shape=jax.ShapeDtypeStruct((n_tok, feats), BF)...]
where the time goes in v3:
time: 153 us; the launch traced here: 152 us
  Pallas kernels  150 us (98%)
  local copies, waits for them, and re-layouts  1.88 us (1%)
    pallas_call x1, Pallas kernels, body(): pl.pallas_call(kernel, out_shape=jax.ShapeDtypeStruct((n_tok, feats), BF)...  150 us

profile of v3, /device:TPU:0, one launch (start us, length us, event | category | flops | bytes accessed | tf_op | source)
XLA Modules:
  0.0 151.5 jit_solution(12355075595176997128)
XLA Ops:
  0.0 149.7 %expert_layer.1 = bf16[128,2048]{1,0:T(8,128)(2,1)} custom-call(s32[8,128]{1,0:T(8,128)} %bitcast.10, f32[8,128]{1,0:T(8,128)} %bitcast.11, s32[1,32]{1,0:T(1,128)} %place_ref.1, bf16[128,2048]{1,0:T(8,128)(2,1)} %bitcast.9, bf16[1,1,4096,512]{3,2,1,0:T(8,128)(2,1)} %wg_hbm.1, bf16[1,1,4096,512]{3,2,1,0:T(8,128)(2,1)} %wu_hbm.1, bf16[1,1,512,4096]{3,2,1,0:T(8,128)(2,1)} %wd_hbm.1), custom_call_target="tpu_custom_call" | custom-call | tf_op jit(solution)/shard_map/expert_layer/pallas_call | solution.py:411
  149.7 1.9 %copy.9 = bf16[1,128,2048]{2,1,0:T(8,128)(2,1)} copy(bf16[1,128,2048]{2,1,0:T(8,128)(2,1)} %bitcast.8) | data formatting | bytes 1048576

commit v4 on v3

--- a/solution.py
+++ b/solution.py
@@ -22,7 +22,7 @@
 def kernel(ids_ref, gates_ref, place_ref, tok, wg_hbm, wu_hbm, wd_hbm, out,
            blocks, aux, pick, spread, first, staged, staged_x, rows, rows_x, acc_g, acc_u, wg, wu, wd, hid, hid_x,
            pair_in, parts,
-           w_sem, aux_s, aux_r, wd_s, wd_r, o_s, o_r, d_s, d_r, l_s, l_r, h_s, h_r, c_s, c_r, x_s, x_r, ready_q):
+           w_sem, wd_load, aux_s, aux_r, wd_s, wd_r, o_s, o_r, d_s, d_r, l_s, l_r, h_s, h_r, c_s, c_r, x_s, x_r, ready_q):
     n_tok, feats = tok.shape
     width = feats // CHUNKS
     experts = place_ref.shape[1]
@@ -84,9 +84,13 @@
     def h_twin(side, k):
         return send(hid.at[k, :, side], hid_x.at[:, k, side], h_s.at[side, k], h_r.at[side, k], twin)
 
-    def c_q(c, side, d):
-        return send(rows.at[c, d, :, side], rows_x.at[c, RING - d, :, side],
-                    c_s.at[side, d - 1, c], c_r.at[side, d - 1, c], q_peer[d])
+    def c_q(c, d):
+        return send(rows.at[c, d, :, 0], rows_x.at[c, RING - d, :, 0],
+                    c_s.at[0, d - 1, c], c_r.at[0, d - 1, c], q_peer[d])
+
+    def c_q_pair(c, h, d):
+        return send(rows.at[c, d, pl.ds(2 * h, 2), 1], rows_x.at[c, RING - d, pl.ds(2 * h, 2), 1],
+                    c_s.at[1 + h, d - 1, c], c_r.at[1 + h, d - 1, c], q_peer[d])
 
     def c_x(c):
         return send(blocks.at[c, 0], pair_in.at[c], x_s.at[RING, c], x_r.at[RING, c], x_side)
@@ -94,11 +98,18 @@
     def c_over(c, d):
         return send(blocks.at[c, 1, d], parts.at[c, d], x_s.at[d, c], x_r.at[d, c], over[d])
 
-    load_g = pltpu.make_async_copy(wg_hbm.at[0, 0], wg, w_sem.at[0])
-    load_u = pltpu.make_async_copy(wu_hbm.at[0, 0], wu, w_sem.at[1])
+    hidden = wd_hbm.shape[2]
+    own_wd, twin_wd = pl.ds(0, hidden), pl.ds(hidden, hidden)
+
+    def load(c, part, which):
+        from_row = ((core + part) % 2) * feats + c * width
+        source, held = ((wg_hbm, wg), (wu_hbm, wu))[which]
+        return pltpu.make_async_copy(source.at[0, 0, pl.ds(pl.multiple_of(from_row, width), width)],
+                                     held.at[c, pl.ds(part * width, width)], w_sem.at[which, part, c])
+
     load_d = pltpu.make_async_copy(
-        wd_hbm.at[0, 0, :, pl.ds(pl.multiple_of(core * feats, feats), feats)], wd.at[0], w_sem.at[2])
-    give_d = send(wd_hbm.at[0, 0, :, pl.ds(pl.multiple_of((1 - core) * feats, feats), feats)], wd.at[1],
+        wd_hbm.at[0, 0, :, pl.ds(pl.multiple_of(core * feats, feats), feats)], wd.at[own_wd], wd_load.at[0])
+    give_d = send(wd_hbm.at[0, 0, :, pl.ds(pl.multiple_of((1 - core) * feats, feats), feats)], wd.at[twin_wd],
                   wd_s.at[0], wd_r.at[0], twin)
 
     for c in range(P_AHEAD):
@@ -139,8 +150,8 @@
             parts_of.append(jnp.where(here, aux[side, b, pl.ds(experts + m, 1), :], 0.0))
         whole = jnp.concatenate(parts_of, axis=0).T
         top = whole.astype(BF)
-        spread[0, side, b] = top
-        spread[1, side, b] = (whole - top.astype(F32)).astype(BF)
+        spread[side, b, :n_tok, :] = top
+        spread[side, b, n_tok:, :] = (whole - top.astype(F32)).astype(BF)
 
     table(0, 0)
     for c in range(CHUNKS):
@@ -154,8 +165,10 @@
             first[d - 1, c] = got[d * CAP:(d + 1) * CAP]
     for d in (2, 1, 3):
         d_first(d).start()
-    load_g.start()
-    load_u.start()
+    for c in range(CHUNKS):
+        for part in range(2):
+            for which in range(2):
+                load(c, part, which).start()
     load_d.start()
     give_d.start()
     for d in range(1, RING):
@@ -170,17 +183,11 @@
     acc_u[...] = jnp.zeros_like(acc_u)
 
     def accumulate(c, side):
-        own = pl.ds(pl.multiple_of(core * feats + c * width, width), width)
-        other = pl.ds(pl.multiple_of((1 - core) * feats + c * width, width), width)
-
-        @pl.loop(0, RING)
-        def _(k):
-            mine = rows[c, k, :, side].reshape(RING * CAP, width)
-            theirs = rows_x[c, k, :, side].reshape(RING * CAP, width)
-            acc_g[side, k] += (jnp.dot(mine, wg[own, :], preferred_element_type=F32)
-                               + jnp.dot(theirs, wg[other, :], preferred_element_type=F32))
-            acc_u[side, k] += (jnp.dot(mine, wu[own, :], preferred_element_type=F32)
-                               + jnp.dot(theirs, wu[other, :], preferred_element_type=F32))
+        many = RING * RING * CAP
+        both = jnp.concatenate([rows[c, :, :, side].reshape(many, width),
+                                rows_x[c, :, :, side].reshape(many, width)], axis=1)
+        for acc, held in ((acc_g, wg), (acc_u, wu)):
+            acc[side] += jnp.dot(both, held[c], preferred_element_type=F32).reshape(acc.shape[1:])
 
     def activate(side):
         for d in range(1, RING):
@@ -193,22 +200,26 @@
             h_twin(side, k).start()
 
     def project(c, side):
-        @pl.loop(0, RING)
-        def _(k):
-            mine = hid[k, :, side].reshape(RING * CAP, hid.shape[-1])
-            theirs = hid_x[k, :, side].reshape(RING * CAP, hid.shape[-1])
-            made = (jnp.dot(mine, wd[0, :, lanes(c)], preferred_element_type=F32)
-                    + jnp.dot(theirs, wd[1, :, lanes(c)], preferred_element_type=F32))
-            rows[c, k, :, side] = made.astype(BF).reshape(RING, CAP, width)
+        many = RING * RING * CAP
+        both = jnp.concatenate([hid[:, :, side].reshape(many, hidden),
+                                hid_x[:, :, side].reshape(many, hidden)], axis=1)
+        made = jnp.dot(both, wd[:, lanes(c)], preferred_element_type=F32)
+        rows[c, :, :, side] = made.astype(BF).reshape(RING, RING, CAP, width)
 
         for d in (2, 1, 3):
-            c_q(c, side, d).start()
+            if side == 0:
+                c_q(c, d).start()
+            else:
+                c_q_pair(c, 1, d).start()
+        if side == 1:
+            for d in (2, 1, 3):
+                c_q_pair(c, 0, d).start()
 
     def spread_out(c, side, b):
         got = jnp.concatenate(
             [rows[c, 0, b, side], rows_x[c, 1, b, side], rows_x[c, 2, b, side], rows_x[c, 3, b, side]], axis=0)
-        return (jnp.dot(spread[0, side, b], got, preferred_element_type=F32)
-                + jnp.dot(spread[1, side, b], got, preferred_element_type=F32))
+        twice = jnp.dot(spread[side, b], got, preferred_element_type=F32)
+        return twice[:n_tok] + twice[n_tok:]
 
     def stage(c, run):
         @pl.when((c >= 0) & (c < CHUNKS))
@@ -283,10 +294,9 @@
             d_twin(c, 1, RING - d).start()
 
     def multiply_own(c):
-        @pl.when(c == 0)
-        def _():
-            load_g.wait()
-            load_u.wait()
+        for part in range(2):
+            for which in range(2):
+                load(c, part, which).wait()
         for k in range(RING):
             d_twin(c, 0, k).wait_recv()
         accumulate(c, 0)
@@ -336,16 +346,17 @@
 
     def add_own(c):
         for d in range(1, RING):
-            c_q(c, 0, d).wait_recv()
+            c_q(c, d).wait_recv()
         for b in range(RING):
             blocks[c, 0, b] = spread_out(c, 0, b).astype(BF)
         c_x(c).start()
 
     def add_other(c):
-        for d in range(1, RING):
-            c_q(c, 1, d).wait_recv()
         c_x(c).wait_recv()
-        for b in (2, 1, 3, 0):
+        for b in (2, 3, 1, 0):
+            if b in (2, 1):
+                for d in range(1, RING):
+                    c_q_pair(c, b // 2, d).wait_recv()
             total = spread_out(c, 1, b) + pair_in[c, b].astype(F32)
             if b == 0:
                 total = total + blocks[c, 1, 0].astype(F32)
@@ -390,8 +401,9 @@
     @pl.loop(0, CHUNKS)
     def _(c):
         for d in range(1, RING):
-            c_q(c, 0, d).wait_send()
-            c_q(c, 1, d).wait_send()
+            c_q(c, d).wait_send()
+            c_q_pair(c, 0, d).wait_send()
+            c_q_pair(c, 1, d).wait_send()
         c_x(c).wait_send()
         for d in range(RING):
             c_over(c, d).wait_send()
@@ -402,7 +414,6 @@
     n_tok, feats = own.shape
     width = feats // CHUNKS
     hidden = w_gate.shape[3]
-    deep = w_gate.shape[2]
     reach = (2, RING, RING * CAP, hidden)
     vmem = pl.BlockSpec(memory_space=pltpu.VMEM)
     anywhere = pl.BlockSpec(memory_space=pl.ANY)
@@ -417,7 +428,7 @@
             held((CHUNKS, 2, RING, n_tok, width), BF),
             held((2, RING, 2 * expert_node.shape[1], n_tok), F32),
             held((2, RING, RING * CAP, n_tok), BF),
-            held((2, 2, RING, n_tok, RING * CAP), BF),
+            held((2, RING, 2 * n_tok, RING * CAP), BF),
             held((RING - 1, CHUNKS, CAP, width), BF),
             held((STAGES, RING - 1, RING - 1, CAP, width), BF),
             held((STAGES, RING - 1, RING, CAP, width), BF),
@@ -425,14 +436,15 @@
             held((CHUNKS, RING, RING, 2, CAP, width), BF),
             held(reach, F32),
             held(reach, F32),
-            held((deep, hidden), BF),
-            held((deep, hidden), BF),
-            held((2, hidden, feats), BF),
+            held((CHUNKS, 2 * width, hidden), BF),
+            held((CHUNKS, 2 * width, hidden), BF),
+            held((2 * hidden, feats), BF),
             held((RING, RING, 2, CAP, hidden), BF),
             held((RING, RING, 2, CAP, hidden), BF),
             held((CHUNKS, RING, n_tok, width), BF),
             held((CHUNKS, RING, n_tok, width), BF),
-            dma((3,)),
+            dma((2, 2, CHUNKS)),
+            dma((1,)),
             dma((RING,)),
             dma((RING,)),
             dma((1,)),
@@ -445,8 +457,8 @@
             dma((2, RING, CHUNKS)),
             dma((2, RING)),
             dma((2, RING)),
-            dma((2, RING - 1, CHUNKS)),
-            dma((2, RING - 1, CHUNKS)),
+            dma((3, RING - 1, CHUNKS)),
+            dma((3, RING - 1, CHUNKS)),
             dma((RING + 1, CHUNKS)),
             dma((RING + 1, CHUNKS)),
             pltpu.SemaphoreType.REGULAR((2,)),

time: 153 us -> 148 us (0.967)
  Pallas kernels: 150 us -> 146 us
    pallas_call x1, Pallas kernels: 150 us -> 146 us  [body(): pl.pallas_call(kernel, out_shape=jax.ShapeDtypeStruct((n_tok, feats), BF)...]
where the time goes in v4:
time: 148 us
  Pallas kernels  146 us (99%)
  local copies, waits for them, and re-layouts  1.88 us (1%)
    pallas_call x1, Pallas kernels, body(): pl.pallas_call(kernel, out_shape=jax.ShapeDtypeStruct((n_tok, feats), BF)...  146 us

profile of v4, /device:TPU:0, one launch (start us, length us, event | category | flops | bytes accessed | tf_op | source)
XLA Modules:
  0.0 147.6 jit_solution(3248348212273490661)
XLA Ops:
  0.0 145.7 %expert_layer.1 = bf16[128,2048]{1,0:T(8,128)(2,1)} custom-call(s32[8,128]{1,0:T(8,128)} %bitcast.10, f32[8,128]{1,0:T(8,128)} %bitcast.11, s32[1,32]{1,0:T(1,128)} %place_ref.1, bf16[128,2048]{1,0:T(8,128)(2,1)} %bitcast.9, bf16[1,1,4096,512]{3,2,1,0:T(8,128)(2,1)} %wg_hbm.1, bf16[1,1,4096,512]{3,2,1,0:T(8,128)(2,1)} %wu_hbm.1, bf16[1,1,512,4096]{3,2,1,0:T(8,128)(2,1)} %wd_hbm.1), custom_call_target="tpu_custom_call" | custom-call | tf_op jit(solution)/shard_map/expert_layer/pallas_call | solution.py:422
  145.7 1.9 %copy.9 = bf16[1,128,2048]{2,1,0:T(8,128)(2,1)} copy(bf16[1,128,2048]{2,1,0:T(8,128)(2,1)} %bitcast.8) | data formatting | bytes 1048576

commit v5 on v4

--- a/solution.py
+++ b/solution.py
@@ -11,6 +11,8 @@
 RING = 4
 CAP = 64
 CHUNKS = 8
+KEEP = 2
+FIRST = 2
 STAGES = 3
 LAG = 2
 SHARE = 1
@@ -21,7 +23,7 @@
 
 def kernel(ids_ref, gates_ref, place_ref, tok, wg_hbm, wu_hbm, wd_hbm, out,
            blocks, aux, pick, spread, first, staged, staged_x, rows, rows_x, acc_g, acc_u, wg, wu, wd, hid, hid_x,
-           pair_in, parts,
+           pair_in, parts, kept,
            w_sem, wd_load, aux_s, aux_r, wd_s, wd_r, o_s, o_r, d_s, d_r, l_s, l_r, h_s, h_r, c_s, c_r, x_s, x_r, ready_q):
     n_tok, feats = tok.shape
     width = feats // CHUNKS
@@ -43,14 +45,14 @@
     q_peer = [None] + [at_node(0, d, 0) for d in range(1, RING)]
     x_side = at_node(0, 0, 1)
     twin = {"node": node, "local": 1 - core, "section": section}
-    over = [at_node(d, 0, 1, 1 - section) for d in range(RING)]
+    over = at_node(0, 0, 1, 1 - section)
 
     def send(src, dst, s, r, to):
         return pltpu.make_async_remote_copy(src_ref=src, dst_ref=dst, send_sem=s, recv_sem=r,
                                             device_id=to, device_id_type=MESH)
 
     barrier = pltpu.get_barrier_semaphore()
-    peers = p_peer[1:] + q_peer[1:] + [x_side, twin] + over
+    peers = p_peer[1:] + q_peer[1:] + [x_side, twin, over]
     for peer in peers:
         pl.semaphore_signal(barrier, inc=1, device_id=peer, device_id_type=MESH)
     pl.semaphore_wait(barrier, len(peers))
@@ -67,8 +69,10 @@
     def d_x(c):
         return send(blocks.at[c, 0, pl.ds(1, 3)], blocks.at[c, 1, pl.ds(1, 3)], d_s.at[4, c], d_r.at[4, c], x_side)
 
-    def d_first(d):
-        return send(first.at[d - 1], rows.at[:, RING - d, 0, 0], o_s.at[d - 1], o_r.at[d - 1], q_peer[d])
+    def d_first(g, d):
+        chunks = pl.ds(g * FIRST, FIRST)
+        return send(first.at[d - 1, chunks], rows.at[chunks, RING - d, 0, 0],
+                    o_s.at[g, d - 1], o_r.at[g, d - 1], q_peer[d])
 
     def d_q(c, d):
         return send(staged.at[c % STAGES, d - 1], rows.at[c, RING - d, pl.ds(1, 3), 0],
@@ -95,8 +99,11 @@
     def c_x(c):
         return send(blocks.at[c, 0], pair_in.at[c], x_s.at[RING, c], x_r.at[RING, c], x_side)
 
-    def c_over(c, d):
-        return send(blocks.at[c, 1, d], parts.at[c, d], x_s.at[d, c], x_r.at[d, c], over[d])
+    def c_p(c, d):
+        return send(blocks.at[c, 1, d], parts.at[c, RING - d - 1], x_s.at[d, c], x_r.at[d, c], p_peer[d])
+
+    def c_over(c):
+        return send(blocks.at[c, 1, 0], out.at[:, lanes(c)], x_s.at[0, c], x_r.at[0, c], over)
 
     hidden = wd_hbm.shape[2]
     own_wd, twin_wd = pl.ds(0, hidden), pl.ds(hidden, hidden)
@@ -142,13 +149,18 @@
     slot_index = lax.broadcasted_iota(jnp.int32, (CAP, n_tok), 0).astype(F32)
 
     def table(side, b):
-        parts_of = []
         for k in range(RING):
             m = p * step_p + ((q + k) % RING) * step_q + x
             here = aux[side, b, pl.ds(m, 1), :] == slot_index
             pick[side, b, k * CAP:(k + 1) * CAP, :] = jnp.where(here, 1.0, 0.0).astype(BF)
-            parts_of.append(jnp.where(here, aux[side, b, pl.ds(experts + m, 1), :], 0.0))
-        whole = jnp.concatenate(parts_of, axis=0).T
+
+    def spread_table(side, b):
+        weights = []
+        for k in range(RING):
+            m = p * step_p + ((q + k) % RING) * step_q + x
+            here = aux[side, b, pl.ds(m, 1), :] == slot_index
+            weights.append(jnp.where(here, aux[side, b, pl.ds(experts + m, 1), :], 0.0))
+        whole = jnp.concatenate(weights, axis=0).T
         top = whole.astype(BF)
         spread[side, b, :n_tok, :] = top
         spread[side, b, n_tok:, :] = (whole - top.astype(F32)).astype(BF)
@@ -163,14 +175,17 @@
         rows[c, 0, 0, 0] = got[:CAP]
         for d in range(1, RING):
             first[d - 1, c] = got[d * CAP:(d + 1) * CAP]
-    for d in (2, 1, 3):
-        d_first(d).start()
+        if c % FIRST == FIRST - 1:
+            for d in (2, 1, 3):
+                d_first(c // FIRST, d).start()
     for c in range(CHUNKS):
         for part in range(2):
             for which in range(2):
                 load(c, part, which).start()
     load_d.start()
     give_d.start()
+    acc_g[...] = jnp.zeros_like(acc_g)
+    acc_u[...] = jnp.zeros_like(acc_u)
     for d in range(1, RING):
         a_p[d].wait_recv()
     a_x.start()
@@ -179,8 +194,6 @@
     def _(b):
         table(0, b)
 
-    acc_g[...] = jnp.zeros_like(acc_g)
-    acc_u[...] = jnp.zeros_like(acc_u)
 
     def accumulate(c, side):
         many = RING * RING * CAP
@@ -282,8 +295,9 @@
     def share_own(c):
         @pl.when(c == 0)
         def _():
-            for d in range(1, RING):
-                d_first(d).wait_recv()
+            for g in range(CHUNKS // FIRST):
+                for d in range(1, RING):
+                    d_first(g, d).wait_recv()
         for d in range(1, RING):
             d_q(c, d).wait_recv()
             d_twin(c, 0, RING - d).start()
@@ -359,16 +373,18 @@
                     c_q_pair(c, b // 2, d).wait_recv()
             total = spread_out(c, 1, b) + pair_in[c, b].astype(F32)
             if b == 0:
-                total = total + blocks[c, 1, 0].astype(F32)
-            blocks[c, 1, b] = total.astype(BF)
-            c_over(c, b).start()
+                kept[c % KEEP] = total + blocks[c, 1, 0].astype(F32)
+            else:
+                blocks[c, 1, b] = total.astype(BF)
+                c_p(c, b).start()
 
     def finish(c):
-        for d in range(RING):
-            c_over(c, d).wait_recv()
-        total = parts[c, 0].astype(F32) + parts[c, 1].astype(F32)
-        total = total + parts[c, 2].astype(F32) + parts[c, 3].astype(F32)
-        out[:, lanes(c)] = total.astype(BF)
+        for d in range(1, RING):
+            c_p(c, d).wait_recv()
+        total = kept[c % KEEP] + parts[c, 0].astype(F32)
+        total = total + parts[c, 1].astype(F32) + parts[c, 2].astype(F32)
+        blocks[c, 1, 0] = total.astype(BF)
+        c_over(c).start()
 
     @pl.loop(0, 2 * CHUNKS + SHARE + ADD + LAG + 2)
     def _(i):
@@ -385,6 +401,11 @@
         stage(j - ADD - LAG, add_other)
         stage(j - ADD - LAG - 1, finish)
 
+        @pl.when((i > LAG) & (i <= LAG + RING))
+        def _():
+            spread_table(0, i - LAG - 1)
+            spread_table(1, i - LAG - 1)
+
     @pl.loop(CHUNKS - STAGES, CHUNKS)
     def _(c):
         for d in range(1, RING):
@@ -392,7 +413,8 @@
             d_qx(c, d).wait_send()
     for d in range(1, RING):
         a_p[d].wait_send()
-        d_first(d).wait_send()
+        for g in range(CHUNKS // FIRST):
+            d_first(g, d).wait_send()
     a_x.wait_send()
     for side in range(2):
         for k in range(RING):
@@ -405,8 +427,9 @@
             c_q_pair(c, 0, d).wait_send()
             c_q_pair(c, 1, d).wait_send()
         c_x(c).wait_send()
-        for d in range(RING):
-            c_over(c, d).wait_send()
+        for d in range(1, RING):
+            c_p(c, d).wait_send()
+        c_over(c).wait()
 
 
 def body(tokens, expert_ids, gate_weights, expert_node, w_gate, w_up, w_down):
@@ -423,7 +446,7 @@
         kernel,
         out_shape=jax.ShapeDtypeStruct((n_tok, feats), BF),
         in_specs=[vmem, vmem, pl.BlockSpec(memory_space=pltpu.SMEM), vmem, anywhere, anywhere, anywhere],
-        out_specs=vmem,
+        out_specs=anywhere,
         scratch_shapes=[
             held((CHUNKS, 2, RING, n_tok, width), BF),
             held((2, RING, 2 * expert_node.shape[1], n_tok), F32),
@@ -442,15 +465,16 @@
             held((RING, RING, 2, CAP, hidden), BF),
             held((RING, RING, 2, CAP, hidden), BF),
             held((CHUNKS, RING, n_tok, width), BF),
-            held((CHUNKS, RING, n_tok, width), BF),
+            held((CHUNKS, RING - 1, n_tok, width), BF),
+            held((KEEP, n_tok, width), F32),
             dma((2, 2, CHUNKS)),
             dma((1,)),
             dma((RING,)),
             dma((RING,)),
             dma((1,)),
             dma((1,)),
-            dma((RING - 1,)),
-            dma((RING - 1,)),
+            dma((CHUNKS // FIRST, RING - 1)),
+            dma((CHUNKS // FIRST, RING - 1)),
             dma((11, CHUNKS)),
             dma((11, CHUNKS)),
             dma((2, RING, CHUNKS)),

time: 148 us -> 145 us (0.980)
  Pallas kernels: 146 us -> 143 us
    pallas_call x1, Pallas kernels: 146 us -> 143 us  [body(): pl.pallas_call(kernel, out_shape=jax.ShapeDtypeStruct((n_tok, feats), BF)...]
where the time goes in v5:
time: 145 us
  Pallas kernels  143 us (99%)
  local copies, waits for them, and re-layouts  1.88 us (1%)
    pallas_call x1, Pallas kernels, body(): pl.pallas_call(kernel, out_shape=jax.ShapeDtypeStruct((n_tok, feats), BF)...  143 us

profile of v5, /device:TPU:0, one launch (start us, length us, event | category | flops | bytes accessed | tf_op | source)
XLA Modules:
  0.0 144.9 jit_solution(7187504444770290763)
XLA Ops:
  0.0 143.0 %expert_layer.1 = bf16[128,2048]{1,0:T(8,128)(2,1)} custom-call(s32[8,128]{1,0:T(8,128)} %bitcast.10, f32[8,128]{1,0:T(8,128)} %bitcast.11, s32[1,32]{1,0:T(1,128)} %place_ref.1, bf16[128,2048]{1,0:T(8,128)(2,1)} %bitcast.9, bf16[1,1,4096,512]{3,2,1,0:T(8,128)(2,1)} %wg_hbm.1, bf16[1,1,4096,512]{3,2,1,0:T(8,128)(2,1)} %wu_hbm.1, bf16[1,1,512,4096]{3,2,1,0:T(8,128)(2,1)} %wd_hbm.1), custom_call_target="tpu_custom_call" | custom-call | tf_op jit(solution)/shard_map/expert_layer/pallas_call | solution.py:445
  143.0 1.9 %copy.9 = bf16[1,128,2048]{2,1,0:T(8,128)(2,1)} copy(bf16[1,128,2048]{2,1,0:T(8,128)(2,1)} %bitcast.8) | data formatting | bytes 1048576
